TPU v7x, 512 devices: a whole 4x8x8 slice. The times are simulated.
512 devices in a mesh: fsdp: 64 (over x, y, core), tp: 8 (over z).
Axes of the slice: x: 4, y: 8, z: 8, core: 2. Of those that a mesh axis runs over, the one named last changes fastest.
Arguments:
- momentum: bfloat16 [28672, 8192], P('fsdp', 'tp'), may hold values from -6 to 6
- gradient: bfloat16 [28672, 8192], P('fsdp', 'tp'), may hold values from -150 to 150, as said below
- right_factor: bfloat16 [8, 1024, 512], P('tp', 'fsdp'), may hold values from -0.0625 to 0.0625
- weight: bfloat16 [28672, 8192], P('fsdp', 'tp'), may hold values from -6 to 6
Outputs:
- momentum_new: bfloat16 [28672, 8192], P('fsdp', 'tp')
- factor_new: bfloat16 [8, 1024, 512], P('tp', 'fsdp')
- weight_new: bfloat16 [28672, 8192], P('fsdp', 'tp')
Inputs may be any that keep to these rules, and one draw needn't show every extreme that they name: `gradient`: Real-valued entries.
All inputs are finite; a program needn't handle non-finite values.
Results may differ from a plain program's by a relative error of at most 0.009.
Values may be sent and summed in bfloat16 or wider, within the bound.
A program may use at most 64 MiB of HBM per device.

v0:
```python
import jax
import jax.numpy as jnp
from jax import lax
from jax.sharding import PartitionSpec as P

D = 8192
FF = 28672
RANK = 512


def left_factor(sketch, gram):
    lower = jnp.linalg.cholesky(gram)
    return jax.scipy.linalg.solve_triangular(lower, sketch.T, lower=True).T


def gram_of(sketch):
    return lax.dot_general(
        sketch, sketch, (((0,), (0,)), ((), ())), precision=lax.Precision.HIGHEST
    )


def local(momentum, gradient, right_factor, weight):
    buffer = (momentum.astype(jnp.float32) + gradient.astype(jnp.float32)).astype(jnp.bfloat16)
    row_count = buffer.shape[0]
    shard_rows = right_factor.shape[1]
    rank_width = right_factor.shape[2]
    local_factor = right_factor[0]
    columns = buffer
    partial_sketch = jnp.dot(
        columns,
        lax.all_gather(local_factor, "fsdp", axis=0, tiled=True),
        preferred_element_type=jnp.float32,
    )
    sketch = lax.psum(partial_sketch, "tp")
    gram = lax.psum(gram_of(sketch), "fsdp")
    left = left_factor(sketch, gram)
    left_half = left.astype(jnp.bfloat16)
    columns = buffer
    rows_share = lax.psum_scatter(
        lax.dot_general(
            columns, left_half, (((0,), (0,)), ((), ())), preferred_element_type=jnp.float32
        ),
        "fsdp",
        scatter_dimension=0,
        tiled=True,
    )
    squares = jnp.sum(rows_share * rows_share, axis=0)
    norms = jnp.sqrt(lax.psum(squares, ("fsdp", "tp")) + 1e-06)
    new_share = (rows_share / norms).astype(jnp.bfloat16)
    stacked = jnp.concatenate([left_half, (left / norms).astype(jnp.bfloat16)], axis=0)
    products = jnp.dot(
        stacked,
        lax.all_gather(rows_share.astype(jnp.bfloat16), "fsdp", axis=0, tiled=True).T,
        preferred_element_type=jnp.float32,
    )
    approx = products[:row_count]
    update = products[row_count:]
    momentum_new = (buffer.astype(jnp.float32) - 0.05 * approx).astype(jnp.bfloat16)
    factor_scale = 0.2 * jnp.sqrt(jnp.float32(FF) * jnp.float32(D) / jnp.float32(RANK))
    weight_new = (weight.astype(jnp.float32) - factor_scale * update).astype(jnp.bfloat16)
    return (momentum_new, new_share.reshape(1, shard_rows, rank_width), weight_new)


def solution(mesh):
    return jax.shard_map(
        local,
        mesh=mesh,
        in_specs=(P("fsdp", "tp"), P("fsdp", "tp"), P("tp", "fsdp", None), P("fsdp", "tp")),
        out_specs=(P("fsdp", "tp"), P("tp", "fsdp", None), P("fsdp", "tp")),
        check_vma=False,
    )
```

profile of v0, /device:TPU:1, one launch (start us, length us, event | category | flops | bytes accessed | tf_op | source)
XLA Modules:
  0.0 857.3 jit_solution(12291485071022287233)
XLA Ops:
  7.2 0.0 all-gather.6.cloned.1.call-start
  7.2 0.7 all-gather.6.cloned.1.call-update
  7.9 0.0 all-reduce.4.cloned.1.call-start
  7.9 90.9 %all-gather.6.cloned.1.call-done = bf16[1,1024,512]{2,1,0:T(8,128)(2,1)} async-done(((bf16[1,16,512]{2,1,0:T(8,128)(2,1)}), bf16[1,1024,512]{2,1,0:T(8,128)(2,1)}) %all-gather.6.cloned.1.call-update) | async-done | bytes 1048592 | tf_op jit(solution)/shard_map/all_gather | solution.py:31
  98.9 3.4 fusion.5
  102.2 0.0 all-reduce.4.cloned.1.call-update
  102.3 0.0 all-reduce.6.cloned.1.call-start
  102.3 75.3 %all-reduce.4.cloned.1.call-done = f32[448,512]{1,0:T(8,128)} async-done(((f32[448,512]{1,0:T(8,128)}), f32[448,512]{1,0:T(8,128)}) %all-reduce.4.cloned.1.call-update) | async-done | bytes 917520 | tf_op jit(solution)/shard_map/psum | solution.py:34
  177.6 4.4 fusion.48
  182.0 0.2 reduce-scatter.2.cloned.1.call-start
  182.3 196.4 %all-reduce.6.cloned.1.call-done = f32[512,512]{0,1:T(8,128)} async-done(((f32[512,512]{0,1:T(8,128)}), f32[512,512]{0,1:T(8,128)}) %all-reduce.6.cloned.1.call-update) | async-done | bytes 1048592 | tf_op jit(solution)/shard_map/psum | solution.py:35
  378.7 1.6 copy.8
  380.3 0.2 fusion.4
  380.6 11.7 %cholesky.104 = f32[128,128]{1,0:T(8,128)S(1)} custom-call(f32[128,128]{1,0:T(8,128)S(1)} %cholesky.266), custom_call_target="Cholesky" | custom-call | tf_op jit(solution)/shard_map/jit(cholesky)/cholesky | solution.py:12
  392.3 9.8 %custom-call.31 = f32[1,128,128]{1,2,0:T(8,128)S(1)} custom-call(f32[1,128,128]{2,1,0:T(8,128)S(1)} %get-tuple-element.32), custom_call_target="InvertDiagBlocksLowerTriangular" | custom-call | tf_op jit(solution)/shard_map/jit(cholesky)/cholesky | solution.py:12
  402.2 0.1 cholesky.224
  402.3 0.3 constant_dynamic-update-slice_fusion.3
  402.6 0.3 convolution_subtract_fusion.3
  402.9 11.7 %cholesky.217 = f32[128,128]{1,0:T(8,128)S(1)} custom-call(f32[128,128]{1,0:T(8,128)S(1)} %cholesky.270), custom_call_target="Cholesky" | custom-call | tf_op jit(solution)/shard_map/jit(cholesky)/cholesky | solution.py:12
  414.7 10.0 %custom-call.32 = f32[1,128,128]{1,2,0:T(8,128)S(1)} custom-call(f32[1,128,128]{2,1,0:T(8,128)S(1)} %get-tuple-element.29), custom_call_target="InvertDiagBlocksLowerTriangular" | custom-call | tf_op jit(solution)/shard_map/jit(cholesky)/cholesky | solution.py:12
  424.7 0.3 convolution_dynamic-update-slice_fusion
  425.0 0.4 convolution_subtract_fusion.4
  425.4 11.7 %cholesky.238 = f32[128,128]{1,0:T(8,128)S(1)} custom-call(f32[128,128]{1,0:T(8,128)S(1)} %cholesky.275), custom_call_target="Cholesky" | custom-call | tf_op jit(solution)/shard_map/jit(cholesky)/cholesky | solution.py:12
  437.1 0.7 compare_reduce_fusion.1
  437.8 9.8 %custom-call.33 = f32[1,128,128]{1,2,0:T(8,128)S(1)} custom-call(f32[1,128,128]{2,1,0:T(8,128)S(1)} %get-tuple-element.26), custom_call_target="InvertDiagBlocksLowerTriangular" | custom-call | tf_op jit(solution)/shard_map/jit(cholesky)/cholesky | solution.py:12
  447.7 0.2 convolution_dynamic-update-slice_fusion.1
  447.9 0.4 convolution_subtract_fusion.5
  448.3 11.7 %cholesky.255 = f32[128,128]{1,0:T(8,128)S(1)} custom-call(f32[128,128]{1,0:T(8,128)S(1)} %convolution_subtract_fusion.5), custom_call_target="Cholesky" | custom-call | tf_op jit(solution)/shard_map/jit(cholesky)/cholesky | solution.py:12
  460.0 0.6 compare_reduce_fusion
  460.6 0.6 compare_reduce_fusion.2
  463.8 0.4 select_select_fusion
  464.2 8.0 while.1
  464.2 0.1 constant_dynamic-slice_fusion.2
  464.3 0.5 fusion.58
  464.8 1.4 bitcast_dynamic-update-slice_fusion.2
  466.2 0.1 constant_dynamic-slice_fusion.2
  466.3 0.5 fusion.58
  466.8 1.4 bitcast_dynamic-update-slice_fusion.2
  468.2 0.1 constant_dynamic-slice_fusion.2
  468.3 0.5 fusion.58
  468.8 1.4 bitcast_dynamic-update-slice_fusion.2
  470.2 0.1 constant_dynamic-slice_fusion.2
  470.3 0.5 fusion.58
  470.8 1.4 bitcast_dynamic-update-slice_fusion.2
  472.3 39.3 %custom-call.34 = f32[4,128,128]{1,2,0:T(8,128)S(1)} custom-call(f32[4,128,128]{2,1,0:T(8,128)S(1)} %get-tuple-element.10), custom_call_target="InvertDiagBlocksLowerTriangular" | custom-call | tf_op jit(solution)/shard_map/jit(_solve_triangular)/triangular_solve | solution.py:13
  511.6 0.3 fusion.22
  512.0 1.2 convolution_subtract_fusion.2
  513.2 0.3 fusion.34
  513.5 1.6 convolution_subtract_fusion.1
  515.1 1.2 fusion.32
  516.3 1.7 convolution_subtract_fusion
  518.0 1.2 fusion.31
  519.2 2.1 fusion.44
  521.3 0.0 all-gather.4.cloned.1.call-start
  521.4 143.0 %reduce-scatter.2.cloned.1.call-done = f32[16,512]{1,0:T(8,128)} async-done(((f32[1024,512]{1,0:T(8,128)}), f32[16,512]{1,0:T(8,128)}) %reduce-scatter.2.cloned.1.call-update) | async-done | bytes 32784 | tf_op jit(solution)/shard_map/reduce_scatter | solution.py:39
  664.4 0.8 multiply_reduce_fusion
  665.1 101.8 %psum.23 = f32[512]{0:T(512)S(1)} all-reduce(f32[512]{0:T(512)S(1)} %multiply_reduce_fusion), channel_id=1, replica_groups=mesh['fsdp'=64,'tp'=8] {'fsdp','tp'}, use_global_device_ids=true, to_apply=%region_12.13 | all-reduce | flops 512 | bytes 4096 | tf_op jit(solution)/shard_map/psum | solution.py:48
  767.0 1.5 fusion.40
  768.4 0.0 all-gather.4.cloned.1.call-update
  768.5 0.8 fusion.46
  769.3 0.8 fusion.20
  770.1 75.9 %all-gather.4.cloned.1.call-done = bf16[1024,512]{1,0:T(8,128)(2,1)} async-done(((bf16[16,512]{1,0:T(8,128)(2,1)}), bf16[1024,512]{1,0:T(8,128)(2,1)}) %all-gather.4.cloned.1.call-update) | async-done | bytes 1048592 | tf_op jit(solution)/shard_map/all_gather | solution.py:53
  846.0 2.7 fusion.7
  848.7 2.0 fusion.1
  (27 shorter events, 0.3 us)
Async XLA Ops:
  7.2 91.7 %all-gather.6.cloned.1.call-start = ((), (), s32[]{:S(2)}) async-start(), calls=%async_computation.5 | async-start | bytes 1064960 | tf_op jit(solution)/shard_map/all_gather | solution.py:31
  7.9 169.7 %all-reduce.4.cloned.1.call-start = ((), (), s32[]{:S(2)}) async-start(), calls=%async_computation.1 | async-start | bytes 1835008 | tf_op jit(solution)/shard_map/psum | solution.py:34
  102.3 276.4 %all-reduce.6.cloned.1.call-start = ((), (), s32[]{:S(2)}) async-start(), calls=%async_computation.2 | async-start | bytes 2097152 | tf_op jit(solution)/shard_map/psum | solution.py:35
  182.0 482.3 %reduce-scatter.2.cloned.1.call-start = ((), (), s32[]{:S(2)}) async-start(), calls=%async_computation.3 | async-start | bytes 2129920 | tf_op jit(solution)/shard_map/reduce_scatter | solution.py:39
  378.7 1.7 copy-start.3
  437.1 74.5 %copy-start = (f32[448,512]{1,0:T(8,128)S(1)}, f32[448,512]{1,0:T(8,128)}, u32[]{:S(2)}) copy-start(f32[448,512]{1,0:T(8,128)} %all-reduce.4.cloned.1.call-done) | copy-start | bytes 2752516
  472.2 39.3 %copy-start.4 = (f32[512,512]{1,0:T(8,128)}, f32[512,512]{1,0:T(8,128)S(1)}, u32[]{:S(2)}) copy-start(f32[512,512]{1,0:T(8,128)S(1)} %get-tuple-element.94) | copy-start | bytes 3145732
  511.6 1.6 copy-start.6
  513.5 5.7 copy-start.1
  513.5 5.6 copy-start.2
  521.3 324.7 %all-gather.4.cloned.1.call-start = ((), (), s32[]{:S(2)}) async-start(), calls=%async_computation.4 | async-start | bytes 1064960 | tf_op jit(solution)/shard_map/all_gather | solution.py:53
  770.1 78.6 %copy-start.5 = (bf16[448,1024]{1,0:T(8,128)(2,1)S(1)}, bf16[448,1024]{1,0:T(8,128)(2,1)}, u32[]{:S(2)}) copy-start(bf16[448,1024]{1,0:T(8,128)(2,1)} %param.7) | copy-start | bytes 2752516
Sparse Core Ops, SparseCore 0:
  11.4 87.4 all-gather.5
  102.4 75.2 all-reduce.3
  182.2 196.4 all-reduce.5
  521.5 142.8 reduce-scatter.1
  768.6 77.3 all-gather.3
where the time goes:
time: 858 us; the launch traced here: 857 us
  waiting for transfers between devices  582 us (68%)
  other arithmetic  124 us (14%)
  blocking collectives  102 us (12%)
  matrix products  21.9 us (3%)
  between operations  16.6 us (2%)
  local copies, waits for them, and re-layouts  9.74 us (1%)
    psum x1, waiting for transfers between devices, local(): gram = lax.psum(gram_of(sketch), 'fsdp')  196 us
    reduce_scatter x1, waiting for transfers between devices, local(): lax.psum_scatter(lax.dot_general(columns, left_half, (((0,), (0,)), ((),...  143 us
    psum x1, blocking collectives, local(): norms = jnp.sqrt(lax.psum(squares, ('fsdp', 'tp')) + 1e-06)  102 us
    all_gather x1, waiting for transfers between devices, local(): lax.all_gather(local_factor, 'fsdp', axis=0, tiled=True)  90.9 us
    another operation x14, other arithmetic, left_factor(): lower = jnp.linalg.cholesky(gram)  78.6 us
    all_gather x1, waiting for transfers between devices, local(): lax.all_gather(rows_share.astype(jnp.bfloat16), 'fsdp', axis=0, tiled=True)  75.9 us
    psum x1, waiting for transfers between devices, local(): sketch = lax.psum(partial_sketch, 'tp')  75.3 us
    another operation x3, other arithmetic, left_factor(): return jax.scipy.linalg.solve_triangular(lower, sketch.T, lower=True).T  39.7 us
  transfers between devices with their start and end apart: 5, of which 5 were waited for; matrix products, arithmetic and copies ran while one was open for 0% of the time, Pallas kernels for 0%

commit v1 on v0

v1 whole, which is shorter than its diff:
```python
import functools

import jax
import jax.numpy as jnp
from jax import lax
from jax.experimental import pallas as pl
from jax.experimental.pallas import tpu as pltpu
from jax.sharding import PartitionSpec as P

D = 8192
FF = 28672
RANK = 512
NX, NY, NC, NZ = 4, 8, 2, 8
ROWS = FF // (NX * NY * NC)
COLS = D // NZ
SHARE = COLS // (NX * NY * NC)
ZR = ROWS // NZ
MESH = pl.DeviceIdType.MESH
HI = lax.Precision.HIGHEST
F32 = jnp.float32
BF16 = jnp.bfloat16

PHASES = {}
_n = 0
for _name, _k in (
    ("fy", 7), ("fx", 3), ("fc", 4), ("sz", 7), ("sg", 7),
    ("gc", 1), ("gx", 3), ("gy", 7), ("gz", 7), ("hy", 7), ("hx", 3), ("hc", 4),
    ("pc", 1), ("px", 3), ("py", 7), ("qy", 7), ("qx", 3), ("qc", 4), ("nz", 7),
):
    PHASES[_name] = _n
    _n += _k
N_SEMS = _n


def wide(x):
    return jnp.broadcast_to(x, (8, 128))


def diag_inverse(m):
    lane = lax.broadcasted_iota(jnp.int32, (8, 128), 1)
    sub = lax.broadcasted_iota(jnp.int32, (8, 128), 0)
    m = list(m)
    n = len(m)
    out = []
    for k in range(n):
        lo = 8 * k
        v = m[k]
        inside = (lane >= lo) & (lane < lo + 8)
        cols = [wide(v[:, lo + j : lo + j + 1]) for j in range(8)]
        a = [[wide(cols[j][i : i + 1, :]) if j <= i else None for j in range(8)] for i in range(8)]
        vi = jnp.where(inside, jnp.where(lane - lo == sub, 1.0, 0.0), v)
        vb = [wide(vi[j : j + 1, :]) for j in range(8)]
        rs = [None] * 8
        r = [None] * 8
        for j in range(8):
            rs[j] = lax.rsqrt(a[j][j])
            r[j] = vb[j] * rs[j]
            for i in range(j + 1, 8):
                a[i][j] = a[i][j] * rs[j]
            for i in range(j + 1, 8):
                for c in range(j + 1, i + 1):
                    a[i][c] = a[i][c] - a[i][j] * a[c][j]
                vb[i] = vb[i] - a[i][j] * r[j]
        q = [None] * 8
        acc = list(r)
        for j in range(7, -1, -1):
            q[j] = acc[j] * rs[j]
            for i in range(j):
                acc[i] = acc[i] - a[j][i] * q[j]
        row = r[0]
        for j in range(1, 8):
            row = jnp.where(sub == j, r[j], row)
        out.append(row)
        for i in range(k + 1, n):
            base = jnp.where(inside, 0.0, m[i])
            t = [wide(m[i][:, lo + j : lo + j + 1]) * q[j] for j in range(8)]
            s = ((t[0] + t[1]) + (t[2] + t[3])) + ((t[4] + t[5]) + (t[6] + t[7]))
            m[i] = base - s
    return out


def split(x):
    hi = x.astype(BF16)
    return hi, (x - hi.astype(F32)).astype(BF16)


def dot_nt(a, b):
    return lax.dot_general(a, b, (((1,), (1,)), ((), ())), preferred_element_type=F32)


def dot_tn(a, b, precision=None):
    return lax.dot_general(
        a, b, (((0,), (0,)), ((), ())), precision=precision, preferred_element_type=F32
    )


def kernel(
    m_hbm, g_hbm, f_hbm, w_hbm,
    mo_hbm, fo_hbm, wo_hbm,
    m_v, g_v, w_v, b_v, f_v, sk_v, skr_v, so_v, sa_v, sh_v, sl_v,
    gs_v, gm_v, gcr_v, gxr_v, g1_v, gyr_v, gzr_v, gg_v, ch_v, dd_v,
    ps_v, pm_v, pcr_v, pxr_v, p1_v, pyr_v, pf_v,
    xh_v, xl_v, le_v, lh_v, ph_v, nz_v, fo_v,
    send_sem, recv_sem, local_sem,
):
    i = lax.axis_index("fsdp")
    z = lax.axis_index("tp")
    c = lax.rem(i, NC)
    y = lax.rem(i // NC, NY)
    x = i // (NC * NY)

    def at(x_, y_, c_):
        return (x_ * NY + y_) * NC + c_

    def around(v, d, n):
        return lax.rem(v + d, n)

    def remote(phase, k, src, dst, fsdp, tp):
        s = PHASES[phase] + k
        return pltpu.make_async_remote_copy(
            src_ref=src, dst_ref=dst, send_sem=send_sem.at[s], recv_sem=recv_sem.at[s],
            device_id=(fsdp, tp), device_id_type=MESH,
        )

    xs = [around(x, d, NX) for d in range(NX)]
    ys = [around(y, d, NY) for d in range(NY)]
    zs = [around(z, d, NZ) for d in range(NZ)]
    other = at(x, y, 1 - c)

    def to_x(phase, src, dst):
        return [remote(phase, d - 1, src(xs[d], d), dst(xs[d], d), at(xs[d], y, c), z) for d in range(1, NX)]

    def to_y(phase, src, dst):
        return [remote(phase, d - 1, src(ys[d], d), dst(ys[d], d), at(x, ys[d], c), z) for d in range(1, NY)]

    def to_z(phase, src, dst):
        return [remote(phase, d - 1, src(zs[d], d), dst(zs[d], d), i, zs[d]) for d in range(1, NZ)]

    def to_core(phase, src, dst):
        return [remote(phase, 0, src, dst, other, z)]

    def rows(ref, start, size):
        return ref.at[pl.ds(pl.multiple_of(start, 8), size)]

    f_mine = f_v.at[x, :, c]
    fy = to_y("fy", lambda p, d: f_hbm.at[0], lambda p, d: f_v.at[x, y, c])
    fx = to_x("fx", lambda p, d: f_mine, lambda p, d: f_mine)
    fc = [
        remote("fc", d, f_v.at[around(x, NX - d, NX), :, c], f_v.at[around(x, NX - d, NX), :, c], other, z)
        for d in range(NX)
    ]
    sz = to_z("sz", lambda p, d: rows(sk_v, p * ZR, ZR), lambda p, d: skr_v.at[d - 1])
    sg = to_z("sg", lambda p, d: so_v, lambda p, d: rows(sa_v, z * ZR, ZR))
    gc = to_core("gc", gs_v, gcr_v)
    gx = to_x("gx", lambda p, d: rows(gm_v, p * 64, 64), lambda p, d: gxr_v.at[d - 1])
    gy = to_y("gy", lambda p, d: rows(g1_v, p * 8, 8), lambda p, d: gyr_v.at[d - 1])
    gz = to_z("gz", lambda p, d: gzr_v.at[z], lambda p, d: gzr_v.at[z])
    g_y = rows(gg_v, c * 256 + x * 64 + y * 8, 8)
    hy = to_y("hy", lambda p, d: g_y, lambda p, d: g_y)
    g_x = rows(gg_v, c * 256 + x * 64, 64)
    hx = to_x("hx", lambda p, d: g_x, lambda p, d: g_x)
    hc = []
    for d in range(NX):
        piece = rows(gg_v, c * 256 + around(x, NX - d, NX) * 64, 64)
        hc.append(remote("hc", d, piece, piece, other, z))
    pc = to_core("pc", ps_v, pcr_v)
    px = to_x("px", lambda p, d: rows(pm_v, p * 128, 128), lambda p, d: pxr_v.at[d - 1])
    py = to_y("py", lambda p, d: rows(p1_v, p * 16, 16), lambda p, d: pyr_v.at[d - 1])
    p_y = rows(pf_v, c * 512 + x * 128 + y * 16, 16)
    qy = to_y("qy", lambda p, d: p_y, lambda p, d: p_y)
    p_x = rows(pf_v, c * 512 + x * 128, 128)
    qx = to_x("qx", lambda p, d: p_x, lambda p, d: p_x)
    qc = []
    for d in range(NX):
        piece = rows(pf_v, c * 512 + around(x, NX - d, NX) * 128, 128)
        qc.append(remote("qc", d, piece, piece, other, z))
    nz = to_z("nz", lambda p, d: nz_v.at[z], lambda p, d: nz_v.at[z])

    def start(copies):
        for k in copies:
            k.start()

    def landed(copies):
        for k in copies:
            k.wait_recv()

    load_m = pltpu.make_async_copy(m_hbm, m_v, local_sem.at[0])
    load_g = pltpu.make_async_copy(g_hbm, g_v, local_sem.at[1])
    load_f = pltpu.make_async_copy(f_hbm.at[0], f_v.at[x, y, c], local_sem.at[2])
    load_w = pltpu.make_async_copy(w_hbm, w_v, local_sem.at[3])
    load_f.start()
    load_m.start()
    load_g.start()
    load_w.start()

    barrier = pltpu.get_barrier_semaphore()
    peers = (
        [(at(xs[d], y, c), z) for d in range(1, NX)]
        + [(at(x, ys[d], c), z) for d in range(1, NY)]
        + [(i, zs[d]) for d in range(1, NZ)]
        + [(other, z)]
    )
    for peer in peers:
        pl.semaphore_signal(barrier, inc=1, device_id=peer, device_id_type=MESH)
    pl.semaphore_wait(barrier, len(peers))

    start(fy)
    load_m.wait()
    load_g.wait()

    def add_buffer(k, _):
        r = pl.ds(pl.multiple_of(k * 64, 64), 64)
        b_v[r, :] = (m_v[r, :].astype(F32) + g_v[r, :].astype(F32)).astype(BF16)
        return 0

    lax.fori_loop(0, ROWS // 64, add_buffer, 0)
    load_f.wait()
    landed(fy)
    start(fx)
    fc[0].start()
    for d in range(1, NX):
        fx[d - 1].wait_recv()
        fc[d].start()
    landed(fc)

    def sketch_rows(k, _):
        r = pl.ds(pl.multiple_of(k * 64, 64), 64)
        sk_v[r, :] = jnp.dot(b_v[r, :], f_v[...].reshape(COLS, RANK), preferred_element_type=F32)
        return 0

    lax.fori_loop(0, ROWS // 64, sketch_rows, 0)
    start(sz)
    total = sk_v[pl.ds(pl.multiple_of(z * ZR, 8), ZR), :]
    for d in range(1, NZ):
        sz[d - 1].wait_recv()
        total = total + skr_v[d - 1]
    so_v[...] = total
    start(sg)
    sa_v[pl.ds(pl.multiple_of(z * ZR, 8), ZR), :] = total

    far = pl.ds(pl.multiple_of((1 - c) * 256, 256), 256)
    near = pl.ds(pl.multiple_of(c * 256, 256), 256)
    gs_v[...] = dot_tn(so_v[:, far], so_v[...], HI)
    start(gc)
    gm_v[...] = dot_tn(so_v[:, near], so_v[...], HI)
    landed(gc)
    gm_v[...] = gm_v[...] + gcr_v[...]
    start(gx)
    total = gm_v[pl.ds(pl.multiple_of(x * 64, 64), 64), :]
    for d in range(1, NX):
        gx[d - 1].wait_recv()
        total = total + gxr_v[d - 1]
    g1_v[...] = total
    start(gy)
    total = g1_v[pl.ds(pl.multiple_of(y * 8, 8), 8), :]
    for d in range(1, NY):
        gy[d - 1].wait_recv()
        total = total + gyr_v[d - 1]
    gzr_v[z] = total
    start(gz)

    landed(sg)

    def split_rows(k, _):
        r = pl.ds(pl.multiple_of(k * 64, 64), 64)
        hi, lo = split(sa_v[r, :])
        sh_v[r, :] = hi
        sl_v[r, :] = lo
        return 0

    lax.fori_loop(0, ROWS // 64, split_rows, 0)

    def project(half, out):
        def tile(k, _):
            cols = pl.ds(pl.multiple_of(half * 512 + k * 128, 128), 128)
            out[pl.ds(pl.multiple_of(k * 128, 128), 128), :] = dot_tn(b_v[:, cols], sh_v[...]) + dot_tn(
                b_v[:, cols], sl_v[...]
            )
            return 0

        lax.fori_loop(0, 4, tile, 0)

    project(1 - c, ps_v)
    start(pc)
    landed(gz)
    total = gzr_v[0]
    for d in range(1, NZ):
        total = total + gzr_v[d]
    gg_v[pl.ds(pl.multiple_of(c * 256 + x * 64 + y * 8, 8), 8), :] = total
    start(hy)
    project(c, pm_v)
    landed(hy)
    start(hx)
    hc[0].start()
    for d in range(1, NX):
        hx[d - 1].wait_recv()
        hc[d].start()

    landed(pc)

    def add_half(k, _):
        r = pl.ds(pl.multiple_of(k * 64, 64), 64)
        pm_v[r, :] = pm_v[r, :] + pcr_v[r, :]
        return 0

    lax.fori_loop(0, 8, add_half, 0)
    start(px)
    landed(hc)

    def progress(step):
        if step == 0:
            total = pm_v[pl.ds(pl.multiple_of(x * 128, 128), 128), :]
            for d in range(1, NX):
                px[d - 1].wait_recv()
                total = total + pxr_v[d - 1]
            p1_v[...] = total
            start(py)
        elif step == 1:
            total = p1_v[pl.ds(pl.multiple_of(y * 16, 16), 16), :]
            for d in range(1, NY):
                py[d - 1].wait_recv()
                total = total + pyr_v[d - 1]
            pf_v[pl.ds(pl.multiple_of(c * 512 + x * 128 + y * 16, 16), 16), :] = total
            start(qy)
        elif step == 2:
            landed(qy)
            start(qx)
            qc[0].start()
        elif step == 3:
            for d in range(1, NX):
                qx[d - 1].wait_recv()
                qc[d].start()

    nb = RANK // 128

    def copy_gram(k, _):
        r = pl.ds(pl.multiple_of(k * 64, 64), 64)
        ch_v[r, :] = gg_v[r, :]
        return 0

    lax.fori_loop(0, 8, copy_gram, 0)

    def eliminate(k, _):
        off = pl.multiple_of(k * 128, 128)
        mine = pl.ds(off, 128)
        blk = ch_v[mine, mine]
        done = diag_inverse([blk[8 * j : 8 * j + 8, :] for j in range(16)])
        for j in range(16):
            dd_v[8 * j : 8 * j + 8, :] = done[j]
        for step in range(4):
            @pl.when(k == step)
            def _():
                progress(step)
        r128 = lax.broadcasted_iota(jnp.int32, (128, 128), 0)
        c128 = lax.broadcasted_iota(jnp.int32, (128, 128), 1)
        linv = jnp.where(r128 >= c128, dd_v[...], 0.0)
        ch_v[mine, mine] = jnp.where(r128 == c128, 1.0, 0.0)
        r = jnp.dot(linv, ch_v[mine, :], precision=HI, preferred_element_type=F32)
        ch_v[mine, :] = r

        def update(k2, _):
            theirs = pl.ds(pl.multiple_of(k2 * 128, 128), 128)
            u = ch_v[mine, theirs]
            ch_v[theirs, mine] = jnp.zeros((128, 128), F32)
            ch_v[theirs, :] = ch_v[theirs, :] - dot_tn(u, r, HI)
            return 0

        lax.fori_loop(k + 1, nb, update, 0)
        return 0

    lax.fori_loop(0, nb, eliminate, 0)

    def split_inverse(k, _):
        r = pl.ds(pl.multiple_of(k * 64, 64), 64)
        rr = lax.broadcasted_iota(jnp.int32, (64, RANK), 0) + k * 64
        cc = lax.broadcasted_iota(jnp.int32, (64, RANK), 1)
        hi, lo = split(jnp.where(rr >= cc, ch_v[r, :], 0.0))
        xh_v[r, :] = hi
        xl_v[r, :] = lo
        return 0

    lax.fori_loop(0, 8, split_inverse, 0)

    landed(qc)
    for copies in (qy, qx, qc):
        for k in copies:
            k.wait_send()
    nz_v[z] = jnp.zeros((8, RANK), F32)

    def projected_rows(k, _):
        r = pl.ds(pl.multiple_of(k * 128, 128), 128)
        hi, lo = split(pf_v[r, :])
        p = dot_nt(hi, xh_v[...]) + (dot_nt(hi, xl_v[...]) + dot_nt(lo, xh_v[...]))
        pf_v[r, :] = p
        ph_v[r, :] = p.astype(BF16)
        nz_v[z] = nz_v[z] + jnp.sum((p * p).reshape(16, 8, RANK), axis=0)
        return 0

    lax.fori_loop(0, COLS // 128, projected_rows, 0)
    start(nz)

    def left_rows(k, _):
        r = pl.ds(pl.multiple_of(k * 64, 64), 64)
        hi, lo = sh_v[r, :], sl_v[r, :]
        left = dot_nt(hi, xh_v[...]) + (dot_nt(hi, xl_v[...]) + dot_nt(lo, xh_v[...]))
        le_v[r, :] = left
        lh_v[r, :] = left.astype(BF16)
        return 0

    lax.fori_loop(0, ROWS // 64, left_rows, 0)

    def momentum_rows(k, _):
        r = pl.ds(pl.multiple_of(k * 64, 64), 64)
        approx = dot_nt(lh_v[r, :], ph_v[...])
        m_v[r, :] = (b_v[r, :].astype(F32) - 0.05 * approx).astype(BF16)
        return 0

    lax.fori_loop(0, ROWS // 64, momentum_rows, 0)
    store_m = pltpu.make_async_copy(m_v, mo_hbm, local_sem.at[0])
    store_m.start()

    landed(nz)
    total = nz_v[0]
    for d in range(1, NZ):
        total = total + nz_v[d]
    inv = 1.0 / jnp.sqrt(jnp.sum(total, axis=0, keepdims=True) + 1e-06)
    fo_v[0] = (pf_v[pl.ds(pl.multiple_of(i * SHARE, SHARE), SHARE), :] * inv).astype(BF16)
    store_f = pltpu.make_async_copy(fo_v, fo_hbm, local_sem.at[2])
    store_f.start()
    load_w.wait()
    scale = 0.2 * (FF * D / RANK) ** 0.5

    def weight_rows(k, _):
        r = pl.ds(pl.multiple_of(k * 64, 64), 64)
        scaled = (le_v[r, :] * inv).astype(BF16)
        w_v[r, :] = (w_v[r, :].astype(F32) - scale * dot_nt(scaled, ph_v[...])).astype(BF16)
        return 0

    lax.fori_loop(0, ROWS // 64, weight_rows, 0)
    store_w = pltpu.make_async_copy(w_v, wo_hbm, local_sem.at[3])
    store_w.start()

    for copies in (fy, fx, fc, sz, sg, gc, gx, gy, gz, hy, hx, hc, pc, px, py, nz):
        for k in copies:
            k.wait_send()
    store_m.wait()
    store_f.wait()
    store_w.wait()


def local(momentum, gradient, right_factor, weight):
    any_spec = pl.BlockSpec(memory_space=pl.ANY)
    v = pltpu.VMEM
    return pl.pallas_call(
        kernel,
        out_shape=(
            jax.ShapeDtypeStruct((ROWS, COLS), BF16),
            jax.ShapeDtypeStruct((1, SHARE, RANK), BF16),
            jax.ShapeDtypeStruct((ROWS, COLS), BF16),
        ),
        in_specs=[any_spec] * 4,
        out_specs=(any_spec,) * 3,
        scratch_shapes=[
            v((ROWS, COLS), BF16), v((ROWS, COLS), BF16), v((ROWS, COLS), BF16), v((ROWS, COLS), BF16),
            v((NX, NY, NC, SHARE, RANK), BF16),
            v((ROWS, RANK), F32), v((7, ZR, RANK), F32), v((ZR, RANK), F32), v((ROWS, RANK), F32),
            v((ROWS, RANK), BF16), v((ROWS, RANK), BF16),
            v((256, RANK), F32), v((256, RANK), F32), v((256, RANK), F32),
            v((3, 64, RANK), F32), v((64, RANK), F32), v((7, 8, RANK), F32), v((8, 8, RANK), F32),
            v((RANK, RANK), F32), v((RANK, RANK), F32), v((128, 128), F32),
            v((512, RANK), F32), v((512, RANK), F32), v((512, RANK), F32),
            v((3, 128, RANK), F32), v((128, RANK), F32), v((7, 16, RANK), F32), v((COLS, RANK), F32),
            v((RANK, RANK), BF16), v((RANK, RANK), BF16),
            v((ROWS, RANK), F32), v((ROWS, RANK), BF16), v((COLS, RANK), BF16),
            v((8, 8, RANK), F32), v((1, SHARE, RANK), BF16),
            pltpu.SemaphoreType.DMA((N_SEMS,)),
            pltpu.SemaphoreType.DMA((N_SEMS,)),
            pltpu.SemaphoreType.DMA((4,)),
        ],
        compiler_params=pltpu.CompilerParams(
            collective_id=0, has_side_effects=True, vmem_limit_bytes=48 * 2**20
        ),
        name="dion_step",
    )(momentum, gradient, right_factor, weight)


def solution(mesh):
    return jax.shard_map(
        local,
        mesh=mesh,
        in_specs=(P("fsdp", "tp"), P("fsdp", "tp"), P("tp", "fsdp", None), P("fsdp", "tp")),
        out_specs=(P("fsdp", "tp"), P("tp", "fsdp", None), P("fsdp", "tp")),
        check_vma=False,
    )
```

time: 858 us -> 163 us (0.19)
  waiting for transfers between devices: 582 us -> 0 us
  Pallas kernels: 0 us -> 155 us
  other arithmetic: 124 us -> 0 us
  blocking collectives: 102 us -> 0 us
  matrix products: 21.9 us -> 0 us
  between operations: 16.6 us -> 0.65 us
    psum x2 -> x0, waiting for transfers between devices: 272 us -> none  [the longest x1 196 us: local(): gram = lax.psum(gram_of(sketch), 'fsdp')]
    all_gather x2 -> x0, waiting for transfers between devices: 167 us -> none  [the longest x1 90.9 us: local(): lax.all_gather(local_factor, 'fsdp', axis=0, tiled=True)]
    pallas_call x0 -> x1, Pallas kernels: none -> 155 us  [local(): pl.pallas_call(kernel, out_shape=(jax.ShapeDtypeStruct((ROWS, COLS), BF16...]
    reduce_scatter x1 -> x0, waiting for transfers between devices: 143 us -> none  [local(): lax.psum_scatter(lax.dot_general(columns, left_half, (((0,), (0,)), ((),...]
    another operation x17 -> x0, other arithmetic: 118 us -> none  [the longest x14 78.6 us: left_factor(): lower = jnp.linalg.cholesky(gram)]
    psum x1 -> x0, blocking collectives: 102 us -> none  [local(): norms = jnp.sqrt(lax.psum(squares, ('fsdp', 'tp')) + 1e-06)]
    dot_general x4 -> x0, matrix products: 12.5 us -> none  [the longest x1 4.37 us: gram_of(): lax.dot_general(sketch, sketch, (((0,), (0,)), ((), ())), precision=lax.P...]
    another operation x13 -> x0, matrix products: 9.33 us -> none  [the longest x7 7.45 us: left_factor(): return jax.scipy.linalg.solve_triangular(lower, sketch.T, lower=True).T]
  transfers between devices with their start and end apart: 5 -> 0, of which waited for: 5 -> 0; matrix products, arithmetic and copies ran while one was open for 0% -> 0% of each run, Pallas kernels for 0% -> 0%
where the time goes in v1:
time: 163 us; the launch traced here: 162 us
  Pallas kernels  155 us (95%)
  local copies, waits for them, and re-layouts  6.7 us (4%)
    pallas_call x1, Pallas kernels, local(): pl.pallas_call(kernel, out_shape=(jax.ShapeDtypeStruct((ROWS, COLS), BF16...  155 us
    unnamed x11, local copies, waits for them, and re-layouts  6.7 us

profile of v1, /device:TPU:1, one launch (start us, length us, event | category | flops | bytes accessed | tf_op | source)
XLA Modules:
  0.0 162.3 jit_solution(2971732662040527610)
XLA Ops:
  0.6 0.0 copy-start
  0.6 1.2 copy-done
  1.8 0.0 copy-start.1
  1.8 1.2 copy-done.1
  3.0 0.0 copy-start.2
  3.0 1.2 copy-done.2
  4.2 0.0 copy-start.3
  4.2 0.7 copy-done.3
  4.9 154.9 %dion_step.1 = (bf16[448,1024]{1,0:T(8,128)(2,1)S(1)}, bf16[1,16,512]{2,1,0:T(8,128)(2,1)S(1)}, bf16[448,1024]{1,0:T(8,128)(2,1)S(1)}) custom-call(bf16[448,1024]{1,0:T(8,128)(2,1)S(1)} %copy-done, bf16[448,1024]{1,0:T(8,128)(2,1)S(1)} %copy-done.1, bf16[1,16,512]{2,1,0:T(8,128)(2,1)S(1)} %copy-done.3, bf16[448,1024]{1,0:T(8,128)(2,1)S(1)} %copy-done.2), custom_call_target="tpu_custom_call" | custom-call | tf_op jit(solution)/shard_map/dion_step/pallas_call | solution.py:454
  159.8 0.9 copy.10
  160.8 0.6 copy.11
  161.4 0.9 copy.12
Async XLA Ops:
  0.6 1.2 copy-start
  1.8 1.2 copy-start.1
  3.0 1.2 copy-start.2
  4.2 0.7 copy-start.3

commit v2 on v1

v2 whole, which is shorter than its diff:
```python
import functools

import jax
import jax.numpy as jnp
from jax import lax
from jax.experimental import pallas as pl
from jax.experimental.pallas import tpu as pltpu
from jax.sharding import PartitionSpec as P

D = 8192
FF = 28672
RANK = 512
NX, NY, NC, NZ = 4, 8, 2, 8
ROWS = FF // (NX * NY * NC)
COLS = D // NZ
SHARE = COLS // (NX * NY * NC)
ZR = ROWS // NZ
MESH = pl.DeviceIdType.MESH
HI = lax.Precision.HIGHEST
F32 = jnp.float32
BF16 = jnp.bfloat16

PHASES = {}
_n = 0
for _name, _k in (
    ("fy", 7), ("fx", 6), ("fc", 4), ("sz", 14), ("sg", 7),
    ("gc", 1), ("gx", 6), ("gy", 7), ("gz", 7), ("hy", 7), ("hx", 6), ("hc", 4),
    ("pc", 1), ("px", 6), ("py", 7), ("qy", 7), ("qx", 6), ("qc", 4), ("nz", 7),
):
    PHASES[_name] = _n
    _n += _k
N_SEMS = _n


def wide(x):
    return jnp.broadcast_to(x, (8, 128))


def diag_inverse(m, between):
    lane = lax.broadcasted_iota(jnp.int32, (8, 128), 1)
    sub = lax.broadcasted_iota(jnp.int32, (8, 128), 0)

    def pick(rows):
        row = rows[0]
        for j in range(1, 8):
            row = jnp.where(sub == j, rows[j], row)
        return row

    m = list(m)
    n = len(m)
    out = []
    for k in range(n):
        between(k)
        lo = 8 * k
        v = m[k]
        inside = (lane >= lo) & (lane < lo + 8)
        cols = [wide(v[:, lo + j : lo + j + 1]) for j in range(8)]
        a = [[wide(cols[j][i : i + 1, :]) if j <= i else None for j in range(8)] for i in range(8)]
        vi = jnp.where(inside, jnp.where(lane - lo == sub, 1.0, 0.0), v)
        vb = [wide(vi[j : j + 1, :]) for j in range(8)]
        near = range(k + 1, min(n, k + 3))
        far = k + 3
        nx = [[wide(m[b][:, lo + j : lo + j + 1]) for j in range(8)] for b in near]
        nl = [[None] * 8 for _ in near]
        new = [jnp.where(inside, 0.0, m[b]) for b in near]
        rs = [None] * 8
        r = [None] * 8
        for j in range(8):
            rs[j] = lax.rsqrt(a[j][j])
            r[j] = vb[j] * rs[j]
            for b in range(len(near)):
                nl[b][j] = nx[b][j] * rs[j]
            for i in range(j + 1, 8):
                a[i][j] = a[i][j] * rs[j]
            for i in range(j + 1, 8):
                for c in range(j + 1, i + 1):
                    a[i][c] = a[i][c] - a[i][j] * a[c][j]
                vb[i] = vb[i] - a[i][j] * r[j]
                for b in range(len(near)):
                    nx[b][i] = nx[b][i] - a[i][j] * nl[b][j]
            for b in range(len(near)):
                new[b] = new[b] - nl[b][j] * r[j]
        out.append(pick(r))
        if far < n:
            q = [None] * 8
            acc = list(r)
            for j in range(7, -1, -1):
                q[j] = acc[j] * rs[j]
                for i in range(j):
                    acc[i] = acc[i] - a[j][i] * q[j]
            padded = [jnp.zeros((8, 128), F32)] * n
            padded[k] = pick(q)
            t = jnp.dot(
                jnp.concatenate(m[far:], axis=0), jnp.concatenate(padded, axis=0),
                precision=HI, preferred_element_type=F32,
            )
            for i in range(far, n):
                m[i] = jnp.where(inside, 0.0, m[i]) - t[8 * (i - far) : 8 * (i - far) + 8, :]
        for b, i in enumerate(near):
            m[i] = new[b]
    return out


def split(x):
    hi = x.astype(BF16)
    return hi, (x - hi.astype(F32)).astype(BF16)


def dot_nt(a, b):
    return lax.dot_general(a, b, (((1,), (1,)), ((), ())), preferred_element_type=F32)


def dot_tn(a, b, precision=None):
    return lax.dot_general(
        a, b, (((0,), (0,)), ((), ())), precision=precision, preferred_element_type=F32
    )


def kernel(
    m_hbm, g_hbm, f_hbm, w_hbm,
    mo_hbm, fo_hbm, wo_hbm,
    m_v, g_v, w_v, b_v, f_v, sk_v, up_v, dn_v, so_v, sa_v, sh_v, sl_v,
    gs_v, gm_v, gcr_v, gxr_v, g1_v, gyr_v, gzr_v, gg_v, ch_v,
    ps_v, pm_v, pcr_v, pxr_v, p1_v, pyr_v, pf_v,
    xh_v, xl_v, le_v, lh_v, ph_v, nz_v, fo_v,
    send_sem, recv_sem, local_sem,
):
    i = lax.axis_index("fsdp")
    z = lax.axis_index("tp")
    c = lax.rem(i, NC)
    y = lax.rem(i // NC, NY)
    x = i // (NC * NY)

    def at(x_, y_, c_):
        return (x_ * NY + y_) * NC + c_

    def around(v, d, n):
        return lax.rem(v + d, n)

    def remote(phase, k, src, dst, fsdp, tp):
        s = PHASES[phase] + k
        return pltpu.make_async_remote_copy(
            src_ref=src, dst_ref=dst, send_sem=send_sem.at[s], recv_sem=recv_sem.at[s],
            device_id=(fsdp, tp), device_id_type=MESH,
        )

    xs = [around(x, d, NX) for d in range(NX)]
    ys = [around(y, d, NY) for d in range(NY)]
    zs = [around(z, d, NZ) for d in range(NZ)]
    other = at(x, y, 1 - c)

    def to_y(phase, src, dst):
        return [remote(phase, d - 1, src(ys[d], d), dst(ys[d], d), at(x, ys[d], c), z) for d in range(1, NY)]

    def to_z(phase, src, dst):
        return [remote(phase, d - 1, src(zs[d], d), dst(zs[d], d), i, zs[d]) for d in range(1, NZ)]

    def to_core(phase, src, dst):
        return [remote(phase, 0, src, dst, other, z)]

    def rows(ref, start, size):
        return ref.at[pl.ds(pl.multiple_of(start, 8), size)]

    def x_sums(phase, src, size, slots):
        half = size // 2

        def a(p):
            return rows(src, p * size, half)

        def b(p):
            return rows(src, p * size + half, half)

        right, left = at(xs[1], y, c), at(xs[3], y, c)
        return [
            remote(phase, 0, a(xs[2]), slots.at[0], right, z),
            remote(phase, 1, b(xs[2]), slots.at[1], left, z),
            remote(phase, 2, b(xs[1]), slots.at[2], right, z),
            remote(phase, 3, a(xs[3]), slots.at[3], left, z),
            remote(phase, 4, slots.at[0], slots.at[4], right, z),
            remote(phase, 5, slots.at[1], slots.at[5], left, z),
        ]

    def x_sums_forward(copies, src, size, slots):
        half = size // 2
        copies[0].wait_recv()
        slots[0] = slots[0] + src[pl.ds(pl.multiple_of(xs[1] * size, 8), half), :]
        copies[4].start()
        copies[1].wait_recv()
        slots[1] = slots[1] + src[pl.ds(pl.multiple_of(xs[3] * size + half, 8), half), :]
        copies[5].start()

    def x_sums_finish(copies, src, size, slots, out):
        half = size // 2
        for k in (2, 3, 4, 5):
            copies[k].wait_recv()
        out[0:half, :] = src[pl.ds(pl.multiple_of(x * size, 8), half), :] + (slots[3] + slots[4])
        out[half:size, :] = src[pl.ds(pl.multiple_of(x * size + half, 8), half), :] + (slots[2] + slots[5])

    def x_all(phase, a, b):
        right, left = at(xs[1], y, c), at(xs[3], y, c)
        return [
            remote(phase, 0, a(x), a(x), right, z),
            remote(phase, 1, b(x), b(x), left, z),
            remote(phase, 2, b(x), b(x), right, z),
            remote(phase, 3, a(x), a(x), left, z),
            remote(phase, 4, a(xs[3]), a(xs[3]), right, z),
            remote(phase, 5, b(xs[1]), b(xs[1]), left, z),
        ]

    def x_all_forward(copies):
        copies[0].wait_recv()
        copies[4].start()
        copies[1].wait_recv()
        copies[5].start()

    def x_all_finish(copies, across):
        copies[2].wait_recv()
        across[0].start()
        copies[3].wait_recv()
        across[1].start()
        copies[4].wait_recv()
        copies[5].wait_recv()
        across[2].start()

    def f_half(h):
        return lambda p: f_v.at[p, pl.ds(h * (NY // 2), NY // 2), c]

    def g_half(h):
        return lambda p: rows(gg_v, c * 256 + p * 64 + h * 32, 32)

    def p_half(h):
        return lambda p: rows(pf_v, c * 512 + p * 128 + h * 64, 64)

    def across(phase, block):
        return [remote(phase, k, block(xs[d]), block(xs[d]), other, z) for k, d in enumerate((0, 3, 1, 2))]

    fy = to_y("fy", lambda p, d: f_hbm.at[0], lambda p, d: f_v.at[x, y, c])
    fx = x_all("fx", f_half(0), f_half(1))
    fc = across("fc", lambda p: f_v.at[p, :, c])

    parts = ((0, 24), (24, 32))
    up, down = [], []
    for s in range(4):
        for h, (first, size) in enumerate(parts):
            src = rows(sk_v, zs[4] * ZR + first, size) if s == 0 else up_v.at[s - 1, pl.ds(first, size)]
            up.append(remote("sz", 2 * s + h, src, up_v.at[s, pl.ds(first, size)], i, zs[1]))
    for s in range(3):
        for h, (first, size) in enumerate(parts):
            src = rows(sk_v, zs[5] * ZR + first, size) if s == 0 else dn_v.at[s - 1, pl.ds(first, size)]
            down.append(remote("sz", 8 + 2 * s + h, src, dn_v.at[s, pl.ds(first, size)], i, zs[7]))
    sg_up = []
    for s in range(4):
        piece = rows(sa_v, zs[(8 - s) % 8] * ZR, ZR)
        sg_up.append(remote("sg", s, so_v if s == 0 else piece, piece, i, zs[1]))
    sg_down = []
    for s in range(3):
        piece = rows(sa_v, zs[s] * ZR, ZR)
        sg_down.append(remote("sg", 4 + s, so_v if s == 0 else piece, piece, i, zs[7]))

    gc = to_core("gc", gs_v, gcr_v)
    gx = x_sums("gx", gm_v, 64, gxr_v)
    gy = to_y("gy", lambda p, d: rows(g1_v, p * 8, 8), lambda p, d: gyr_v.at[d - 1])
    gz = to_z("gz", lambda p, d: gzr_v.at[z], lambda p, d: gzr_v.at[z])
    g_y = rows(gg_v, c * 256 + x * 64 + y * 8, 8)
    hy = to_y("hy", lambda p, d: g_y, lambda p, d: g_y)
    hx = x_all("hx", g_half(0), g_half(1))
    hc = across("hc", lambda p: rows(gg_v, c * 256 + p * 64, 64))
    pc = to_core("pc", ps_v, pcr_v)
    px = x_sums("px", pm_v, 128, pxr_v)
    py = to_y("py", lambda p, d: rows(p1_v, p * 16, 16), lambda p, d: pyr_v.at[d - 1])
    p_y = rows(pf_v, c * 512 + x * 128 + y * 16, 16)
    qy = to_y("qy", lambda p, d: p_y, lambda p, d: p_y)
    qx = x_all("qx", p_half(0), p_half(1))
    qc = across("qc", lambda p: rows(pf_v, c * 512 + p * 128, 128))
    nz = to_z("nz", lambda p, d: nz_v.at[z], lambda p, d: nz_v.at[z])

    def start(copies):
        for k in copies:
            k.start()

    def landed(copies):
        for k in copies:
            k.wait_recv()

    load_m = pltpu.make_async_copy(m_hbm, m_v, local_sem.at[0])
    load_g = pltpu.make_async_copy(g_hbm, g_v, local_sem.at[1])
    load_f = pltpu.make_async_copy(f_hbm.at[0], f_v.at[x, y, c], local_sem.at[2])
    load_w = pltpu.make_async_copy(w_hbm, w_v, local_sem.at[3])
    load_f.start()
    load_m.start()
    load_g.start()
    load_w.start()

    barrier = pltpu.get_barrier_semaphore()
    peers = (
        [(at(xs[d], y, c), z) for d in (1, 3)]
        + [(at(x, ys[d], c), z) for d in range(1, NY)]
        + [(i, zs[d]) for d in range(1, NZ)]
        + [(other, z)]
    )
    for peer in peers:
        pl.semaphore_signal(barrier, inc=1, device_id=peer, device_id_type=MESH)
    pl.semaphore_wait(barrier, len(peers))

    start(fy)
    load_m.wait()
    load_g.wait()

    def add_buffer(k, _):
        r = pl.ds(pl.multiple_of(k * 64, 64), 64)
        b_v[r, :] = (m_v[r, :].astype(F32) + g_v[r, :].astype(F32)).astype(BF16)
        return 0

    lax.fori_loop(0, ROWS // 64, add_buffer, 0)
    load_f.wait()
    landed(fy)
    start(fx[:4])
    fc[0].start()
    x_all_forward(fx)
    x_all_finish(fx, fc[1:])
    landed(fc)

    sk_v[...] = jnp.dot(b_v[...], f_v[...].reshape(COLS, RANK), preferred_element_type=F32)
    start(up[:2])
    start(down[:2])
    for s in range(1, 4):
        for h, (first, size) in enumerate(parts):
            part = pl.ds(first, size)
            up[2 * s - 2 + h].wait_recv()
            mine = pl.ds(pl.multiple_of(zs[4 - s] * ZR + first, 8), size)
            up_v[s - 1, part, :] = up_v[s - 1, part, :] + sk_v[mine, :]
            up[2 * s + h].start()
            if s < 3:
                down[2 * s - 2 + h].wait_recv()
                mine = pl.ds(pl.multiple_of(zs[5 + s] * ZR + first, 8), size)
                dn_v[s - 1, part, :] = dn_v[s - 1, part, :] + sk_v[mine, :]
                down[2 * s + h].start()
    landed(down[4:])
    landed(up[6:])
    total = sk_v[pl.ds(pl.multiple_of(z * ZR, 8), ZR), :] + (up_v[3] + dn_v[2])
    so_v[...] = total
    sg_up[0].start()
    sg_down[0].start()
    sa_v[pl.ds(pl.multiple_of(z * ZR, 8), ZR), :] = total

    def sg_forward(s):
        sg_up[s - 1].wait_recv()
        sg_up[s].start()
        if s < 3:
            sg_down[s - 1].wait_recv()
            sg_down[s].start()

    far = pl.ds(pl.multiple_of((1 - c) * 256, 256), 256)
    near = pl.ds(pl.multiple_of(c * 256, 256), 256)
    gs_v[...] = dot_tn(so_v[:, far], so_v[...], HI)
    start(gc)
    gm_v[...] = dot_tn(so_v[:, near], so_v[...], HI)
    landed(gc)
    gm_v[...] = gm_v[...] + gcr_v[...]
    start(gx[:4])
    sg_forward(1)
    x_sums_forward(gx, gm_v, 64, gxr_v)
    sg_forward(2)
    x_sums_finish(gx, gm_v, 64, gxr_v, g1_v)
    start(gy)
    sg_forward(3)
    total = g1_v[pl.ds(pl.multiple_of(y * 8, 8), 8), :]
    for d in range(1, NY):
        gy[d - 1].wait_recv()
        total = total + gyr_v[d - 1]
    gzr_v[z] = total
    start(gz)

    landed(sg_up[3:])
    landed(sg_down[2:])
    sh_v[...], sl_v[...] = split(sa_v[...])

    def project(half):
        cols = pl.ds(pl.multiple_of(half * 512, 512), 512)
        return dot_tn(b_v[:, cols], sh_v[...]) + dot_tn(b_v[:, cols], sl_v[...])

    ps_v[...] = project(1 - c)
    start(pc)
    landed(gz)
    total = gzr_v[0]
    for d in range(1, NZ):
        total = total + gzr_v[d]
    gg_v[pl.ds(pl.multiple_of(c * 256 + x * 64 + y * 8, 8), 8), :] = total
    start(hy)
    pm_v[...] = project(c)
    landed(hy)
    start(hx[:4])
    hc[0].start()
    landed(pc)
    pm_v[...] = pm_v[...] + pcr_v[...]
    x_all_forward(hx)
    start(px[:4])
    x_all_finish(hx, hc[1:])
    landed(hc)
    x_sums_forward(px, pm_v, 128, pxr_v)

    def progress(step):
        if step == 0:
            x_sums_finish(px, pm_v, 128, pxr_v, p1_v)
            start(py)
        elif step == 1:
            total = p1_v[pl.ds(pl.multiple_of(y * 16, 16), 16), :]
            for d in range(1, NY):
                py[d - 1].wait_recv()
                total = total + pyr_v[d - 1]
            pf_v[pl.ds(pl.multiple_of(c * 512 + x * 128 + y * 16, 16), 16), :] = total
            start(qy)
        elif step == 2:
            landed(qy)
            start(qx[:4])
            qc[0].start()
        elif step == 3:
            x_all_forward(qx)
        elif step == 4:
            x_all_finish(qx, qc[1:])

    nb = RANK // 128

    ch_v[...] = gg_v[...]
    r128 = lax.broadcasted_iota(jnp.int32, (128, 128), 0)
    c128 = lax.broadcasted_iota(jnp.int32, (128, 128), 1)

    def eliminate(k, _):
        mine = pl.ds(pl.multiple_of(k * 128, 128), 128)
        blk = ch_v[mine, mine]

        def between(j):
            for step, (outer, pivot) in enumerate(((0, 5), (1, 5), (2, 5), (2, 11), (3, 8))):
                if j == pivot:

                    @pl.when(k == outer)
                    def _():
                        progress(step)

        done = diag_inverse([blk[8 * j : 8 * j + 8, :] for j in range(16)], between)
        linv = jnp.where(r128 >= c128, jnp.concatenate(done, axis=0), 0.0)
        ch_v[mine, mine] = jnp.where(r128 == c128, 1.0, 0.0)
        ch_v[mine, :] = jnp.dot(linv, ch_v[mine, :], precision=HI, preferred_element_type=F32)
        for kk in range(nb - 1):

            @pl.when(k == kk)
            def _():
                lo, hi = 128 * kk, 128 * (kk + 1)
                ch_v[hi:, lo:hi] = jnp.zeros((RANK - hi, 128), F32)
                ch_v[hi:, :] = ch_v[hi:, :] - dot_tn(ch_v[lo:hi, hi:], ch_v[lo:hi, :], HI)

        return 0

    lax.fori_loop(0, nb, eliminate, 0)
    rr = lax.broadcasted_iota(jnp.int32, (RANK, RANK), 0)
    cc = lax.broadcasted_iota(jnp.int32, (RANK, RANK), 1)
    xh_v[...], xl_v[...] = split(jnp.where(rr >= cc, ch_v[...], 0.0))

    landed(qc)
    for copies in (qy, qx, qc):
        for k in copies:
            k.wait_send()

    def times_inverse(hi, lo):
        return dot_nt(hi, xh_v[...]) + (dot_nt(hi, xl_v[...]) + dot_nt(lo, xh_v[...]))

    proj = times_inverse(*split(pf_v[...]))
    pf_v[...] = proj
    ph_v[...] = proj.astype(BF16)
    nz_v[z] = jnp.sum((proj * proj).reshape(COLS // 8, 8, RANK), axis=0)
    start(nz)

    left = times_inverse(sh_v[...], sl_v[...])
    le_v[...] = left
    lh_v[...] = left.astype(BF16)

    stores = []
    for h in range(2):
        cols = slice(512 * h, 512 * h + 512)
        approx = dot_nt(lh_v[...], ph_v[cols, :])
        m_v[:, cols] = (b_v[:, cols].astype(F32) - 0.05 * approx).astype(BF16)
        stores.append(pltpu.make_async_copy(m_v.at[:, cols], mo_hbm.at[:, cols], local_sem.at[4 + h]))
        stores[-1].start()

    landed(nz)
    total = nz_v[0]
    for d in range(1, NZ):
        total = total + nz_v[d]
    inv = 1.0 / jnp.sqrt(jnp.sum(total, axis=0, keepdims=True) + 1e-06)
    fo_v[0] = (pf_v[pl.ds(pl.multiple_of(i * SHARE, SHARE), SHARE), :] * inv).astype(BF16)
    store_f = pltpu.make_async_copy(fo_v, fo_hbm, local_sem.at[2])
    store_f.start()
    load_w.wait()
    scale = 0.2 * (FF * D / RANK) ** 0.5

    scaled = (le_v[...] * inv).astype(BF16)
    for h in range(2):
        cols = slice(512 * h, 512 * h + 512)
        update = dot_nt(scaled, ph_v[cols, :])
        w_v[:, cols] = (w_v[:, cols].astype(F32) - scale * update).astype(BF16)
        stores.append(pltpu.make_async_copy(w_v.at[:, cols], wo_hbm.at[:, cols], local_sem.at[6 + h]))
        stores[-1].start()

    for copies in (fy, fx, fc, up, down, sg_up, sg_down, gc, gx, gy, gz, hy, hx, hc, pc, px, py, nz):
        for k in copies:
            k.wait_send()
    store_f.wait()
    for store in stores:
        store.wait()


def local(momentum, gradient, right_factor, weight):
    any_spec = pl.BlockSpec(memory_space=pl.ANY)
    v = pltpu.VMEM
    return pl.pallas_call(
        kernel,
        out_shape=(
            jax.ShapeDtypeStruct((ROWS, COLS), BF16),
            jax.ShapeDtypeStruct((1, SHARE, RANK), BF16),
            jax.ShapeDtypeStruct((ROWS, COLS), BF16),
        ),
        in_specs=[any_spec] * 4,
        out_specs=(any_spec,) * 3,
        scratch_shapes=[
            v((ROWS, COLS), BF16), v((ROWS, COLS), BF16), v((ROWS, COLS), BF16), v((ROWS, COLS), BF16),
            v((NX, NY, NC, SHARE, RANK), BF16),
            v((ROWS, RANK), F32), v((4, ZR, RANK), F32), v((3, ZR, RANK), F32), v((ZR, RANK), F32), v((ROWS, RANK), F32),
            v((ROWS, RANK), BF16), v((ROWS, RANK), BF16),
            v((256, RANK), F32), v((256, RANK), F32), v((256, RANK), F32),
            v((6, 32, RANK), F32), v((64, RANK), F32), v((7, 8, RANK), F32), v((8, 8, RANK), F32),
            v((RANK, RANK), F32), v((RANK, RANK), F32),
            v((512, RANK), F32), v((512, RANK), F32), v((512, RANK), F32),
            v((6, 64, RANK), F32), v((128, RANK), F32), v((7, 16, RANK), F32), v((COLS, RANK), F32),
            v((RANK, RANK), BF16), v((RANK, RANK), BF16),
            v((ROWS, RANK), F32), v((ROWS, RANK), BF16), v((COLS, RANK), BF16),
            v((8, 8, RANK), F32), v((1, SHARE, RANK), BF16),
            pltpu.SemaphoreType.DMA((N_SEMS,)),
            pltpu.SemaphoreType.DMA((N_SEMS,)),
            pltpu.SemaphoreType.DMA((8,)),
        ],
        compiler_params=pltpu.CompilerParams(
            collective_id=0, has_side_effects=True, vmem_limit_bytes=60 * 2**20
        ),
        name="dion_step",
    )(momentum, gradient, right_factor, weight)


def solution(mesh):
    return jax.shard_map(
        local,
        mesh=mesh,
        in_specs=(P("fsdp", "tp"), P("fsdp", "tp"), P("tp", "fsdp", None), P("fsdp", "tp")),
        out_specs=(P("fsdp", "tp"), P("tp", "fsdp", None), P("fsdp", "tp")),
        check_vma=False,
    )
```

time: 163 us -> 135 us (0.83)
  Pallas kernels: 155 us -> 130 us
  local copies, waits for them, and re-layouts: 6.7 us -> 3.78 us
    pallas_call x1, Pallas kernels: 155 us -> 130 us  [local(): pl.pallas_call(kernel, out_shape=(jax.ShapeDtypeStruct((ROWS, COLS), BF16...]
    unnamed x11 -> x7, local copies, waits for them, and re-layouts: 6.7 us -> 3.78 us
where the time goes in v2:
time: 135 us
  Pallas kernels  130 us (96%)
  local copies, waits for them, and re-layouts  3.78 us (3%)
    pallas_call x1, Pallas kernels, local(): pl.pallas_call(kernel, out_shape=(jax.ShapeDtypeStruct((ROWS, COLS), BF16...  130 us
    unnamed x7, local copies, waits for them, and re-layouts  3.78 us

profile of v2, /device:TPU:1, one launch (start us, length us, event | category | flops | bytes accessed | tf_op | source)
XLA Modules:
  0.0 134.9 jit_solution(7041239482402059435)
XLA Ops:
  0.6 130.4 %dion_step.1 = (bf16[448,1024]{1,0:T(8,128)(2,1)}, bf16[1,16,512]{2,1,0:T(8,128)(2,1)}, bf16[448,1024]{1,0:T(8,128)(2,1)}) custom-call(bf16[448,1024]{1,0:T(8,128)(2,1)} %m_hbm.1, bf16[448,1024]{1,0:T(8,128)(2,1)} %g_hbm.1, bf16[1,16,512]{2,1,0:T(8,128)(2,1)} %f_hbm.1, bf16[448,1024]{1,0:T(8,128)(2,1)} %w_hbm.1), custom_call_target="tpu_custom_call" | custom-call | tf_op jit(solution)/shard_map/dion_step/pallas_call | solution.py:515
  131.1 0.0 copy-start.1
  131.1 0.0 copy-start
  131.1 2.2 %copy.10 = bf16[448,1024]{1,0:T(8,128)(2,1)} copy(bf16[448,1024]{1,0:T(8,128)(2,1)} %get-tuple-element.6) | data formatting | bytes 1835008
  133.3 0.0 copy-done.1
  133.3 0.6 copy.11
  133.9 0.0 copy-done
  133.9 0.9 copy.12
Async XLA Ops:
  131.1 2.3 %copy-start.1 = (bf16[1,16,512]{2,1,0:T(8,128)(2,1)S(1)}, bf16[1,16,512]{2,1,0:T(8,128)(2,1)}, u32[]{:S(2)}) copy-start(bf16[1,16,512]{2,1,0:T(8,128)(2,1)} %get-tuple-element.7) | copy-start | bytes 49156
  131.1 2.9 %copy-start = (bf16[448,1024]{1,0:T(8,128)(2,1)S(1)}, bf16[448,1024]{1,0:T(8,128)(2,1)}, u32[]{:S(2)}) copy-start(bf16[448,1024]{1,0:T(8,128)(2,1)} %get-tuple-element.8) | copy-start | bytes 2752516

commit v3 on v2

--- a/solution.py
+++ b/solution.py
@@ -15,6 +15,10 @@
 COLS = D // NZ
 SHARE = COLS // (NX * NY * NC)
 ZR = ROWS // NZ
+PANELS = ((0, 0), (0, 128), (0, 256), (0, 384), (256, 256), (256, 384))
+GC = 3 * 256
+GX = GC // NX
+GY = GX // NY
 MESH = pl.DeviceIdType.MESH
 HI = lax.Precision.HIGHEST
 F32 = jnp.float32
@@ -117,12 +121,12 @@
 
 
 def kernel(
-    m_hbm, g_hbm, f_hbm, w_hbm,
-    mo_hbm, fo_hbm, wo_hbm,
-    m_v, g_v, w_v, b_v, f_v, sk_v, up_v, dn_v, so_v, sa_v, sh_v, sl_v,
+    m_hbm, g_hbm, f_hbm,
+    b_hbm, lh_hbm, sc_hbm, ph_hbm, fo_hbm,
+    m_v, g_v, b_v, f_v, sk_v, up_v, dn_v, so_v, sa_v, sh_v, sl_v,
     gs_v, gm_v, gcr_v, gxr_v, g1_v, gyr_v, gzr_v, gg_v, ch_v,
     ps_v, pm_v, pcr_v, pxr_v, p1_v, pyr_v, pf_v,
-    xh_v, xl_v, le_v, lh_v, ph_v, nz_v, fo_v,
+    xh_v, xl_v, le_v, lh_v, sc_v, ph_v, nz_v, fo_v,
     send_sem, recv_sem, local_sem,
 ):
     i = lax.axis_index("fsdp")
@@ -226,7 +230,7 @@
         return lambda p: f_v.at[p, pl.ds(h * (NY // 2), NY // 2), c]
 
     def g_half(h):
-        return lambda p: rows(gg_v, c * 256 + p * 64 + h * 32, 32)
+        return lambda p: rows(gg_v, c * GC + p * GX + h * (GX // 2), GX // 2)
 
     def p_half(h):
         return lambda p: rows(pf_v, c * 512 + p * 128 + h * 64, 64)
@@ -234,7 +238,7 @@
     def across(phase, block):
         return [remote(phase, k, block(xs[d]), block(xs[d]), other, z) for k, d in enumerate((0, 3, 1, 2))]
 
-    fy = to_y("fy", lambda p, d: f_hbm.at[0], lambda p, d: f_v.at[x, y, c])
+    fy = to_y("fy", lambda p, d: f_v.at[x, y, c], lambda p, d: f_v.at[x, y, c])
     fx = x_all("fx", f_half(0), f_half(1))
     fc = across("fc", lambda p: f_v.at[p, :, c])
 
@@ -258,13 +262,13 @@
         sg_down.append(remote("sg", 4 + s, so_v if s == 0 else piece, piece, i, zs[7]))
 
     gc = to_core("gc", gs_v, gcr_v)
-    gx = x_sums("gx", gm_v, 64, gxr_v)
-    gy = to_y("gy", lambda p, d: rows(g1_v, p * 8, 8), lambda p, d: gyr_v.at[d - 1])
+    gx = x_sums("gx", gm_v, GX, gxr_v)
+    gy = to_y("gy", lambda p, d: rows(g1_v, p * GY, GY), lambda p, d: gyr_v.at[d - 1])
     gz = to_z("gz", lambda p, d: gzr_v.at[z], lambda p, d: gzr_v.at[z])
-    g_y = rows(gg_v, c * 256 + x * 64 + y * 8, 8)
+    g_y = rows(gg_v, c * GC + x * GX + y * GY, GY)
     hy = to_y("hy", lambda p, d: g_y, lambda p, d: g_y)
     hx = x_all("hx", g_half(0), g_half(1))
-    hc = across("hc", lambda p: rows(gg_v, c * 256 + p * 64, 64))
+    hc = across("hc", lambda p: rows(gg_v, c * GC + p * GX, GX))
     pc = to_core("pc", ps_v, pcr_v)
     px = x_sums("px", pm_v, 128, pxr_v)
     py = to_y("py", lambda p, d: rows(p1_v, p * 16, 16), lambda p, d: pyr_v.at[d - 1])
@@ -285,11 +289,9 @@
     load_m = pltpu.make_async_copy(m_hbm, m_v, local_sem.at[0])
     load_g = pltpu.make_async_copy(g_hbm, g_v, local_sem.at[1])
     load_f = pltpu.make_async_copy(f_hbm.at[0], f_v.at[x, y, c], local_sem.at[2])
-    load_w = pltpu.make_async_copy(w_hbm, w_v, local_sem.at[3])
     load_f.start()
     load_m.start()
     load_g.start()
-    load_w.start()
 
     barrier = pltpu.get_barrier_semaphore()
     peers = (
@@ -302,6 +304,7 @@
         pl.semaphore_signal(barrier, inc=1, device_id=peer, device_id_type=MESH)
     pl.semaphore_wait(barrier, len(peers))
 
+    load_f.wait()
     start(fy)
     load_m.wait()
     load_g.wait()
@@ -312,7 +315,8 @@
         return 0
 
     lax.fori_loop(0, ROWS // 64, add_buffer, 0)
-    load_f.wait()
+    stores = [pltpu.make_async_copy(b_v, b_hbm, local_sem.at[3])]
+    stores[0].start()
     landed(fy)
     start(fx[:4])
     fc[0].start()
@@ -350,21 +354,27 @@
             sg_down[s - 1].wait_recv()
             sg_down[s].start()
 
-    far = pl.ds(pl.multiple_of((1 - c) * 256, 256), 256)
-    near = pl.ds(pl.multiple_of(c * 256, 256), 256)
-    gs_v[...] = dot_tn(so_v[:, far], so_v[...], HI)
+    def panels(core, out):
+        for j in range(3):
+            n = 3 * core + j
+            last = n // 4
+            r = pl.ds(pl.multiple_of(256 * last, 256), 256)
+            q = pl.ds(pl.multiple_of(128 * n - 256 * last, 128), 128)
+            out[256 * j : 256 * j + 256, :] = dot_tn(so_v[:, r], so_v[:, q], HI)
+
+    panels(1 - c, gs_v)
     start(gc)
-    gm_v[...] = dot_tn(so_v[:, near], so_v[...], HI)
+    panels(c, gm_v)
     landed(gc)
     gm_v[...] = gm_v[...] + gcr_v[...]
     start(gx[:4])
     sg_forward(1)
-    x_sums_forward(gx, gm_v, 64, gxr_v)
+    x_sums_forward(gx, gm_v, GX, gxr_v)
     sg_forward(2)
-    x_sums_finish(gx, gm_v, 64, gxr_v, g1_v)
+    x_sums_finish(gx, gm_v, GX, gxr_v, g1_v)
     start(gy)
     sg_forward(3)
-    total = g1_v[pl.ds(pl.multiple_of(y * 8, 8), 8), :]
+    total = g1_v[pl.ds(pl.multiple_of(y * GY, 8), GY), :]
     for d in range(1, NY):
         gy[d - 1].wait_recv()
         total = total + gyr_v[d - 1]
@@ -381,47 +391,46 @@
 
     ps_v[...] = project(1 - c)
     start(pc)
+    pm_v[...] = project(c)
     landed(gz)
     total = gzr_v[0]
     for d in range(1, NZ):
         total = total + gzr_v[d]
-    gg_v[pl.ds(pl.multiple_of(c * 256 + x * 64 + y * 8, 8), 8), :] = total
+    gg_v[pl.ds(pl.multiple_of(c * GC + x * GX + y * GY, 8), GY), :] = total
     start(hy)
-    pm_v[...] = project(c)
+    landed(pc)
+    pm_v[...] = pm_v[...] + pcr_v[...]
+    start(px[:4])
     landed(hy)
     start(hx[:4])
     hc[0].start()
-    landed(pc)
-    pm_v[...] = pm_v[...] + pcr_v[...]
+    x_sums_forward(px, pm_v, 128, pxr_v)
     x_all_forward(hx)
-    start(px[:4])
+    x_sums_finish(px, pm_v, 128, pxr_v, p1_v)
+    start(py)
     x_all_finish(hx, hc[1:])
     landed(hc)
-    x_sums_forward(px, pm_v, 128, pxr_v)
 
     def progress(step):
         if step == 0:
-            x_sums_finish(px, pm_v, 128, pxr_v, p1_v)
-            start(py)
-        elif step == 1:
             total = p1_v[pl.ds(pl.multiple_of(y * 16, 16), 16), :]
             for d in range(1, NY):
                 py[d - 1].wait_recv()
                 total = total + pyr_v[d - 1]
             pf_v[pl.ds(pl.multiple_of(c * 512 + x * 128 + y * 16, 16), 16), :] = total
             start(qy)
-        elif step == 2:
+        elif step == 1:
             landed(qy)
             start(qx[:4])
             qc[0].start()
-        elif step == 3:
+        elif step == 2:
             x_all_forward(qx)
-        elif step == 4:
-            x_all_finish(qx, qc[1:])
 
     nb = RANK // 128
 
-    ch_v[...] = gg_v[...]
+    ch_v[256:, :256] = jnp.zeros((256, 256), F32)
+    for j, (r, q) in enumerate(PANELS):
+        ch_v[r : r + 256, q : q + 128] = gg_v[256 * j : 256 * j + 256, :]
     r128 = lax.broadcasted_iota(jnp.int32, (128, 128), 0)
     c128 = lax.broadcasted_iota(jnp.int32, (128, 128), 1)
 
@@ -430,7 +439,7 @@
         blk = ch_v[mine, mine]
 
         def between(j):
-            for step, (outer, pivot) in enumerate(((0, 5), (1, 5), (2, 5), (2, 11), (3, 8))):
+            for step, (outer, pivot) in enumerate(((1, 4), (2, 12), (3, 8))):
                 if j == pivot:
 
                     @pl.when(k == outer)
@@ -456,84 +465,87 @@
     cc = lax.broadcasted_iota(jnp.int32, (RANK, RANK), 1)
     xh_v[...], xl_v[...] = split(jnp.where(rr >= cc, ch_v[...], 0.0))
 
+    def times_inverse(hi, lo):
+        return dot_nt(hi, xh_v[...]) + (dot_nt(hi, xl_v[...]) + dot_nt(lo, xh_v[...]))
+
+    def store(src, dst, sem):
+        stores.append(pltpu.make_async_copy(src, dst, local_sem.at[sem]))
+        stores[-1].start()
+
+    left = times_inverse(sh_v[...], sl_v[...])
+    le_v[...] = left
+    lh_v[...] = left.astype(BF16)
+    store(lh_v, lh_hbm, 4)
+
+    x_all_finish(qx, qc[1:])
     landed(qc)
     for copies in (qy, qx, qc):
         for k in copies:
             k.wait_send()
-
-    def times_inverse(hi, lo):
-        return dot_nt(hi, xh_v[...]) + (dot_nt(hi, xl_v[...]) + dot_nt(lo, xh_v[...]))
-
     proj = times_inverse(*split(pf_v[...]))
     pf_v[...] = proj
+    squares = jnp.sum(jnp.sum((proj * proj).reshape(COLS // 8, 8, RANK), axis=0), axis=0, keepdims=True)
+    for j in range(4):
+        nz_v[z, j : j + 1, :] = squares[:, 128 * j : 128 * j + 128]
+    nz_v[z, 4:8, :] = jnp.zeros((4, 128), F32)
+    start(nz)
     ph_v[...] = proj.astype(BF16)
-    nz_v[z] = jnp.sum((proj * proj).reshape(COLS // 8, 8, RANK), axis=0)
-    start(nz)
-
-    left = times_inverse(sh_v[...], sl_v[...])
-    le_v[...] = left
-    lh_v[...] = left.astype(BF16)
-
-    stores = []
-    for h in range(2):
-        cols = slice(512 * h, 512 * h + 512)
-        approx = dot_nt(lh_v[...], ph_v[cols, :])
-        m_v[:, cols] = (b_v[:, cols].astype(F32) - 0.05 * approx).astype(BF16)
-        stores.append(pltpu.make_async_copy(m_v.at[:, cols], mo_hbm.at[:, cols], local_sem.at[4 + h]))
-        stores[-1].start()
+    store(ph_v, ph_hbm, 5)
 
     landed(nz)
     total = nz_v[0]
     for d in range(1, NZ):
         total = total + nz_v[d]
-    inv = 1.0 / jnp.sqrt(jnp.sum(total, axis=0, keepdims=True) + 1e-06)
+    inv = 1.0 / jnp.sqrt(total + 1e-06)
+    inv = jnp.concatenate([inv[j : j + 1, :] for j in range(4)], axis=1)
+    sc_v[...] = (le_v[...] * inv).astype(BF16)
+    store(sc_v, sc_hbm, 6)
     fo_v[0] = (pf_v[pl.ds(pl.multiple_of(i * SHARE, SHARE), SHARE), :] * inv).astype(BF16)
-    store_f = pltpu.make_async_copy(fo_v, fo_hbm, local_sem.at[2])
-    store_f.start()
-    load_w.wait()
-    scale = 0.2 * (FF * D / RANK) ** 0.5
-
-    scaled = (le_v[...] * inv).astype(BF16)
-    for h in range(2):
-        cols = slice(512 * h, 512 * h + 512)
-        update = dot_nt(scaled, ph_v[cols, :])
-        w_v[:, cols] = (w_v[:, cols].astype(F32) - scale * update).astype(BF16)
-        stores.append(pltpu.make_async_copy(w_v.at[:, cols], wo_hbm.at[:, cols], local_sem.at[6 + h]))
-        stores[-1].start()
+    store(fo_v, fo_hbm, 7)
 
     for copies in (fy, fx, fc, up, down, sg_up, sg_down, gc, gx, gy, gz, hy, hx, hc, pc, px, py, nz):
         for k in copies:
             k.wait_send()
-    store_f.wait()
-    for store in stores:
-        store.wait()
+    for k in stores:
+        k.wait()
+
+
+def finish(b_ref, w_ref, lh_ref, sc_ref, ph_ref, f_ref, mo_ref, wo_ref, fo_ref):
+    approx = dot_nt(lh_ref[...], ph_ref[...])
+    mo_ref[...] = (b_ref[...].astype(F32) - 0.05 * approx).astype(BF16)
+    update = dot_nt(sc_ref[...], ph_ref[...])
+    scale = 0.2 * (FF * D / RANK) ** 0.5
+    wo_ref[...] = (w_ref[...].astype(F32) - scale * update).astype(BF16)
+    fo_ref[...] = f_ref[...]
 
 
 def local(momentum, gradient, right_factor, weight):
     any_spec = pl.BlockSpec(memory_space=pl.ANY)
     v = pltpu.VMEM
-    return pl.pallas_call(
+    buffer, left_half, scaled_half, projected_half, factor_new = pl.pallas_call(
         kernel,
         out_shape=(
             jax.ShapeDtypeStruct((ROWS, COLS), BF16),
+            jax.ShapeDtypeStruct((ROWS, RANK), BF16),
+            jax.ShapeDtypeStruct((ROWS, RANK), BF16),
+            jax.ShapeDtypeStruct((COLS, RANK), BF16),
             jax.ShapeDtypeStruct((1, SHARE, RANK), BF16),
-            jax.ShapeDtypeStruct((ROWS, COLS), BF16),
         ),
-        in_specs=[any_spec] * 4,
-        out_specs=(any_spec,) * 3,
+        in_specs=[any_spec] * 3,
+        out_specs=(any_spec,) * 5,
         scratch_shapes=[
-            v((ROWS, COLS), BF16), v((ROWS, COLS), BF16), v((ROWS, COLS), BF16), v((ROWS, COLS), BF16),
+            v((ROWS, COLS), BF16), v((ROWS, COLS), BF16), v((ROWS, COLS), BF16),
             v((NX, NY, NC, SHARE, RANK), BF16),
             v((ROWS, RANK), F32), v((4, ZR, RANK), F32), v((3, ZR, RANK), F32), v((ZR, RANK), F32), v((ROWS, RANK), F32),
             v((ROWS, RANK), BF16), v((ROWS, RANK), BF16),
-            v((256, RANK), F32), v((256, RANK), F32), v((256, RANK), F32),
-            v((6, 32, RANK), F32), v((64, RANK), F32), v((7, 8, RANK), F32), v((8, 8, RANK), F32),
-            v((RANK, RANK), F32), v((RANK, RANK), F32),
+            v((GC, 128), F32), v((GC, 128), F32), v((GC, 128), F32),
+            v((6, GX // 2, 128), F32), v((GX, 128), F32), v((7, GY, 128), F32), v((8, GY, 128), F32),
+            v((2 * GC, 128), F32), v((RANK, RANK), F32),
             v((512, RANK), F32), v((512, RANK), F32), v((512, RANK), F32),
             v((6, 64, RANK), F32), v((128, RANK), F32), v((7, 16, RANK), F32), v((COLS, RANK), F32),
             v((RANK, RANK), BF16), v((RANK, RANK), BF16),
-            v((ROWS, RANK), F32), v((ROWS, RANK), BF16), v((COLS, RANK), BF16),
-            v((8, 8, RANK), F32), v((1, SHARE, RANK), BF16),
+            v((ROWS, RANK), F32), v((ROWS, RANK), BF16), v((ROWS, RANK), BF16), v((COLS, RANK), BF16),
+            v((8, 8, 128), F32), v((1, SHARE, RANK), BF16),
             pltpu.SemaphoreType.DMA((N_SEMS,)),
             pltpu.SemaphoreType.DMA((N_SEMS,)),
             pltpu.SemaphoreType.DMA((8,)),
@@ -542,7 +554,28 @@
             collective_id=0, has_side_effects=True, vmem_limit_bytes=60 * 2**20
         ),
         name="dion_step",
-    )(momentum, gradient, right_factor, weight)
+    )(momentum, gradient, right_factor)
+    tile = 256
+    wide_spec = pl.BlockSpec((ROWS, tile), lambda j: (0, j))
+    left_spec = pl.BlockSpec((ROWS, RANK), lambda j: (0, 0))
+    share_spec = pl.BlockSpec((1, SHARE, RANK), lambda j: (0, 0, 0))
+    momentum_new, weight_new, factor_new = pl.pallas_call(
+        finish,
+        grid=(COLS // tile,),
+        out_shape=(
+            jax.ShapeDtypeStruct((ROWS, COLS), BF16),
+            jax.ShapeDtypeStruct((ROWS, COLS), BF16),
+            jax.ShapeDtypeStruct((1, SHARE, RANK), BF16),
+        ),
+        in_specs=[
+            wide_spec, wide_spec, left_spec, left_spec,
+            pl.BlockSpec((tile, RANK), lambda j: (j, 0)), share_spec,
+        ],
+        out_specs=(wide_spec, wide_spec, share_spec),
+        compiler_params=pltpu.CompilerParams(vmem_limit_bytes=60 * 2**20),
+        name="finish",
+    )(buffer, weight, left_half, scaled_half, projected_half, factor_new)
+    return momentum_new, factor_new, weight_new
 
 
 def solution(mesh):

time: 135 us -> 125 us (0.926)
  Pallas kernels: 130 us -> 124 us
  local copies, waits for them, and re-layouts: 3.78 us -> 0 us
    pallas_call x1, Pallas kernels: 130 us -> 119 us  [local(): pl.pallas_call(kernel, out_shape=(jax.ShapeDtypeStruct((ROWS, COLS), BF16...]
    pallas_call x0 -> x1, Pallas kernels: none -> 5.17 us  [local(): pl.pallas_call(finish, grid=(COLS // tile,), out_shape=(jax.ShapeDtypeStr...]
    unnamed x7 -> x0, local copies, waits for them, and re-layouts: 3.78 us -> none
where the time goes in v3:
time: 125 us
  Pallas kernels  124 us (99%)
    pallas_call x1, Pallas kernels, local(): pl.pallas_call(kernel, out_shape=(jax.ShapeDtypeStruct((ROWS, COLS), BF16...  119 us
    pallas_call x1, Pallas kernels, local(): pl.pallas_call(finish, grid=(COLS // tile,), out_shape=(jax.ShapeDtypeStr...  5.17 us

profile of v3, /device:TPU:1, one launch (start us, length us, event | category | flops | bytes accessed | tf_op | source)
XLA Modules:
  0.0 124.8 jit_solution(5053031531194183424)
XLA Ops:
  0.6 119.0 %dion_step.1 = (bf16[448,1024]{1,0:T(8,128)(2,1)}, bf16[448,512]{1,0:T(8,128)(2,1)}, bf16[448,512]{1,0:T(8,128)(2,1)}, bf16[1024,512]{1,0:T(8,128)(2,1)}, bf16[1,16,512]{2,1,0:T(8,128)(2,1)}) custom-call(bf16[448,1024]{1,0:T(8,128)(2,1)} %m_hbm.1, bf16[448,1024]{1,0:T(8,128)(2,1)} %g_hbm.1, bf16[1,16,512]{2,1,0:T(8,128)(2,1)} %f_hbm.1), custom_call_target="tpu_custom_call" | custom-call | tf_op jit(solution)/shard_map/dion_step/pallas_call | solution.py:525
  119.7 5.2 %finish.1 = (bf16[448,1024]{1,0:T(8,128)(2,1)}, bf16[448,1024]{1,0:T(8,128)(2,1)}, bf16[1,16,512]{2,1,0:T(8,128)(2,1)}) custom-call(bf16[448,1024]{1,0:T(8,128)(2,1)} %get-tuple-element.11.b_ref, bf16[448,1024]{1,0:T(8,128)(2,1)} %w_ref.1, bf16[448,512]{1,0:T(8,128)(2,1)} %get-tuple-element.12.lh_ref, bf16[448,512]{1,0:T(8,128)(2,1)} %get-tuple-element.13.sc_ref, ...), custom_call_target="tpu_custom_call" | custom-call | tf_op jit(solution)/shard_map/finish/pallas_call | solution.py:562

commit v4 on v3

--- a/solution.py
+++ b/solution.py
@@ -15,6 +15,7 @@
 COLS = D // NZ
 SHARE = COLS // (NX * NY * NC)
 ZR = ROWS // NZ
+HR = RANK // 2
 PANELS = ((0, 0), (0, 128), (0, 256), (0, 384), (256, 256), (256, 384))
 GC = 3 * 256
 GX = GC // NX
@@ -29,7 +30,8 @@
 for _name, _k in (
     ("fy", 7), ("fx", 6), ("fc", 4), ("sz", 14), ("sg", 7),
     ("gc", 1), ("gx", 6), ("gy", 7), ("gz", 7), ("hy", 7), ("hx", 6), ("hc", 4),
-    ("pc", 1), ("px", 6), ("py", 7), ("qy", 7), ("qx", 6), ("qc", 4), ("nz", 7),
+    ("pc0", 1), ("px0", 6), ("py0", 7), ("qy0", 7), ("qx0", 6), ("qc0", 4),
+    ("pc1", 1), ("px1", 6), ("py1", 7), ("qy1", 7), ("qx1", 6), ("qc1", 4), ("nz", 7),
 ):
     PHASES[_name] = _n
     _n += _k
@@ -125,7 +127,7 @@
     b_hbm, lh_hbm, sc_hbm, ph_hbm, fo_hbm,
     m_v, g_v, b_v, f_v, sk_v, up_v, dn_v, so_v, sa_v, sh_v, sl_v,
     gs_v, gm_v, gcr_v, gxr_v, g1_v, gyr_v, gzr_v, gg_v, ch_v,
-    ps_v, pm_v, pcr_v, pxr_v, p1_v, pyr_v, pf_v,
+    ps_v, pm_v, pcr_v, pxr_v, p1_v, pyr_v, pf_v, pr_v,
     xh_v, xl_v, le_v, lh_v, sc_v, ph_v, nz_v, fo_v,
     send_sem, recv_sem, local_sem,
 ):
@@ -231,9 +233,6 @@
 
     def g_half(h):
         return lambda p: rows(gg_v, c * GC + p * GX + h * (GX // 2), GX // 2)
-
-    def p_half(h):
-        return lambda p: rows(pf_v, c * 512 + p * 128 + h * 64, 64)
 
     def across(phase, block):
         return [remote(phase, k, block(xs[d]), block(xs[d]), other, z) for k, d in enumerate((0, 3, 1, 2))]
@@ -269,13 +268,22 @@
     hy = to_y("hy", lambda p, d: g_y, lambda p, d: g_y)
     hx = x_all("hx", g_half(0), g_half(1))
     hc = across("hc", lambda p: rows(gg_v, c * GC + p * GX, GX))
-    pc = to_core("pc", ps_v, pcr_v)
-    px = x_sums("px", pm_v, 128, pxr_v)
-    py = to_y("py", lambda p, d: rows(p1_v, p * 16, 16), lambda p, d: pyr_v.at[d - 1])
-    p_y = rows(pf_v, c * 512 + x * 128 + y * 16, 16)
-    qy = to_y("qy", lambda p, d: p_y, lambda p, d: p_y)
-    qx = x_all("qx", p_half(0), p_half(1))
-    qc = across("qc", lambda p: rows(pf_v, c * 512 + p * 128, 128))
+    def projection_copies(j):
+        p_y = rows(pf_v.at[j], c * 512 + x * 128 + y * 16, 16)
+
+        def half(h):
+            return lambda p: rows(pf_v.at[j], c * 512 + p * 128 + h * 64, 64)
+
+        return (
+            to_core(f"pc{j}", ps_v.at[j], pcr_v.at[j]),
+            x_sums(f"px{j}", pm_v.at[j], 128, pxr_v.at[j]),
+            to_y(f"py{j}", lambda p, d: rows(p1_v.at[j], p * 16, 16), lambda p, d: pyr_v.at[j, d - 1]),
+            to_y(f"qy{j}", lambda p, d: p_y, lambda p, d: p_y),
+            x_all(f"qx{j}", half(0), half(1)),
+            across(f"qc{j}", lambda p: rows(pf_v.at[j], c * 512 + p * 128, 128)),
+        )
+
+    pc, px, py, qy, qx, qc = zip(projection_copies(0), projection_copies(1))
     nz = to_z("nz", lambda p, d: nz_v.at[z], lambda p, d: nz_v.at[z])
 
     def start(copies):
@@ -385,46 +393,71 @@
     landed(sg_down[2:])
     sh_v[...], sl_v[...] = split(sa_v[...])
 
-    def project(half):
+    def project(half, j):
         cols = pl.ds(pl.multiple_of(half * 512, 512), 512)
-        return dot_tn(b_v[:, cols], sh_v[...]) + dot_tn(b_v[:, cols], sl_v[...])
-
-    ps_v[...] = project(1 - c)
-    start(pc)
-    pm_v[...] = project(c)
+        part = slice(HR * j, HR * j + HR)
+        return dot_tn(b_v[:, cols], sh_v[:, part]) + dot_tn(b_v[:, cols], sl_v[:, part])
+
+    for j in range(2):
+        ps_v[j] = project(1 - c, j)
+        start(pc[j])
+    for j in range(2):
+        pm_v[j] = project(c, j)
     landed(gz)
     total = gzr_v[0]
     for d in range(1, NZ):
         total = total + gzr_v[d]
     gg_v[pl.ds(pl.multiple_of(c * GC + x * GX + y * GY, 8), GY), :] = total
     start(hy)
-    landed(pc)
-    pm_v[...] = pm_v[...] + pcr_v[...]
-    start(px[:4])
+
+    def px_start(j):
+        landed(pc[j])
+        pm_v[j] = pm_v[j] + pcr_v[j]
+        start(px[j][:4])
+
+    def px_forward(j):
+        x_sums_forward(px[j], pm_v.at[j], 128, pxr_v.at[j])
+
+    def px_finish(j):
+        x_sums_finish(px[j], pm_v.at[j], 128, pxr_v.at[j], p1_v.at[j])
+        start(py[j])
+
+    def py_finish(j):
+        total = p1_v[j, pl.ds(pl.multiple_of(y * 16, 16), 16), :]
+        for d in range(1, NY):
+            py[j][d - 1].wait_recv()
+            total = total + pyr_v[j, d - 1]
+        pf_v[j, pl.ds(pl.multiple_of(c * 512 + x * 128 + y * 16, 16), 16), :] = total
+        start(qy[j])
+
+    def qy_finish(j):
+        landed(qy[j])
+        start(qx[j][:4])
+        qc[j][0].start()
+
+    px_start(0)
+    px_start(1)
+    px_forward(0)
     landed(hy)
     start(hx[:4])
     hc[0].start()
-    x_sums_forward(px, pm_v, 128, pxr_v)
+    px_forward(1)
     x_all_forward(hx)
-    x_sums_finish(px, pm_v, 128, pxr_v, p1_v)
-    start(py)
+    px_finish(0)
     x_all_finish(hx, hc[1:])
+    px_finish(1)
     landed(hc)
 
-    def progress(step):
-        if step == 0:
-            total = p1_v[pl.ds(pl.multiple_of(y * 16, 16), 16), :]
-            for d in range(1, NY):
-                py[d - 1].wait_recv()
-                total = total + pyr_v[d - 1]
-            pf_v[pl.ds(pl.multiple_of(c * 512 + x * 128 + y * 16, 16), 16), :] = total
-            start(qy)
-        elif step == 1:
-            landed(qy)
-            start(qx[:4])
-            qc[0].start()
-        elif step == 2:
-            x_all_forward(qx)
+    steps = (
+        (0, 3, lambda: py_finish(0)),
+        (1, 0, lambda: py_finish(1)),
+        (1, 9, lambda: qy_finish(0)),
+        (2, 6, lambda: x_all_forward(qx[0])),
+        (2, 7, lambda: qy_finish(1)),
+        (2, 14, lambda: x_all_finish(qx[0], qc[0][1:])),
+        (3, 6, lambda: x_all_forward(qx[1])),
+        (3, 14, lambda: x_all_finish(qx[1], qc[1][1:])),
+    )
 
     nb = RANK // 128
 
@@ -439,12 +472,9 @@
         blk = ch_v[mine, mine]
 
         def between(j):
-            for step, (outer, pivot) in enumerate(((1, 4), (2, 12), (3, 8))):
+            for outer, pivot, step in steps:
                 if j == pivot:
-
-                    @pl.when(k == outer)
-                    def _():
-                        progress(step)
+                    pl.when(k == outer)(step)
 
         done = diag_inverse([blk[8 * j : 8 * j + 8, :] for j in range(16)], between)
         linv = jnp.where(r128 >= c128, jnp.concatenate(done, axis=0), 0.0)
@@ -472,25 +502,26 @@
         stores.append(pltpu.make_async_copy(src, dst, local_sem.at[sem]))
         stores[-1].start()
 
+    def projected(half):
+        r = pl.ds(pl.multiple_of(half * 512, 512), 512)
+        proj = times_inverse(*split(jnp.concatenate([pf_v[0, r, :], pf_v[1, r, :]], axis=1)))
+        pr_v[r, :] = proj
+        ph_v[r, :] = proj.astype(BF16)
+        return jnp.sum((proj * proj).reshape(64, 8, RANK), axis=0)
+
+    squares = projected(c)
+    landed(qc[0])
+    landed(qc[1])
+    squares = jnp.sum(squares + projected(1 - c), axis=0, keepdims=True)
+    for j in range(4):
+        nz_v[z, j : j + 1, :] = squares[:, 128 * j : 128 * j + 128]
+    nz_v[z, 4:8, :] = jnp.zeros((4, 128), F32)
+    start(nz)
+    store(ph_v, ph_hbm, 5)
     left = times_inverse(sh_v[...], sl_v[...])
     le_v[...] = left
     lh_v[...] = left.astype(BF16)
     store(lh_v, lh_hbm, 4)
-
-    x_all_finish(qx, qc[1:])
-    landed(qc)
-    for copies in (qy, qx, qc):
-        for k in copies:
-            k.wait_send()
-    proj = times_inverse(*split(pf_v[...]))
-    pf_v[...] = proj
-    squares = jnp.sum(jnp.sum((proj * proj).reshape(COLS // 8, 8, RANK), axis=0), axis=0, keepdims=True)
-    for j in range(4):
-        nz_v[z, j : j + 1, :] = squares[:, 128 * j : 128 * j + 128]
-    nz_v[z, 4:8, :] = jnp.zeros((4, 128), F32)
-    start(nz)
-    ph_v[...] = proj.astype(BF16)
-    store(ph_v, ph_hbm, 5)
 
     landed(nz)
     total = nz_v[0]
@@ -500,10 +531,10 @@
     inv = jnp.concatenate([inv[j : j + 1, :] for j in range(4)], axis=1)
     sc_v[...] = (le_v[...] * inv).astype(BF16)
     store(sc_v, sc_hbm, 6)
-    fo_v[0] = (pf_v[pl.ds(pl.multiple_of(i * SHARE, SHARE), SHARE), :] * inv).astype(BF16)
+    fo_v[0] = (pr_v[pl.ds(pl.multiple_of(i * SHARE, SHARE), SHARE), :] * inv).astype(BF16)
     store(fo_v, fo_hbm, 7)
 
-    for copies in (fy, fx, fc, up, down, sg_up, sg_down, gc, gx, gy, gz, hy, hx, hc, pc, px, py, nz):
+    for copies in (fy, fx, fc, up, down, sg_up, sg_down, gc, gx, gy, gz, hy, hx, hc, *pc, *px, *py, *qy, *qx, *qc, nz):
         for k in copies:
             k.wait_send()
     for k in stores:
@@ -541,8 +572,9 @@
             v((GC, 128), F32), v((GC, 128), F32), v((GC, 128), F32),
             v((6, GX // 2, 128), F32), v((GX, 128), F32), v((7, GY, 128), F32), v((8, GY, 128), F32),
             v((2 * GC, 128), F32), v((RANK, RANK), F32),
-            v((512, RANK), F32), v((512, RANK), F32), v((512, RANK), F32),
-            v((6, 64, RANK), F32), v((128, RANK), F32), v((7, 16, RANK), F32), v((COLS, RANK), F32),
+            v((2, 512, HR), F32), v((2, 512, HR), F32), v((2, 512, HR), F32),
+            v((2, 6, 64, HR), F32), v((2, 128, HR), F32), v((2, 7, 16, HR), F32), v((2, COLS, HR), F32),
+            v((COLS, RANK), F32),
             v((RANK, RANK), BF16), v((RANK, RANK), BF16),
             v((ROWS, RANK), F32), v((ROWS, RANK), BF16), v((ROWS, RANK), BF16), v((COLS, RANK), BF16),
             v((8, 8, 128), F32), v((1, SHARE, RANK), BF16),
@@ -555,7 +587,7 @@
         ),
         name="dion_step",
     )(momentum, gradient, right_factor)
-    tile = 256
+    tile = 512
     wide_spec = pl.BlockSpec((ROWS, tile), lambda j: (0, j))
     left_spec = pl.BlockSpec((ROWS, RANK), lambda j: (0, 0))
     share_spec = pl.BlockSpec((1, SHARE, RANK), lambda j: (0, 0, 0))

time: 125 us -> 122 us (0.976)
  Pallas kernels: 124 us -> 122 us
    pallas_call x1, Pallas kernels: 119 us -> 118 us  [local(): pl.pallas_call(kernel, out_shape=(jax.ShapeDtypeStruct((ROWS, COLS), BF16...]
where the time goes in v4:
time: 122 us
  Pallas kernels  122 us (100%)
    pallas_call x1, Pallas kernels, local(): pl.pallas_call(kernel, out_shape=(jax.ShapeDtypeStruct((ROWS, COLS), BF16...  118 us
    pallas_call x1, Pallas kernels, local(): pl.pallas_call(finish, grid=(COLS // tile,), out_shape=(jax.ShapeDtypeStr...  3.94 us

profile of v4, /device:TPU:1, one launch (start us, length us, event | category | flops | bytes accessed | tf_op | source)
XLA Modules:
  0.0 122.3 jit_solution(6529894722100091577)
XLA Ops:
  0.6 117.7 %dion_step.1 = (bf16[448,1024]{1,0:T(8,128)(2,1)}, bf16[448,512]{1,0:T(8,128)(2,1)}, bf16[448,512]{1,0:T(8,128)(2,1)}, bf16[1024,512]{1,0:T(8,128)(2,1)}, bf16[1,16,512]{2,1,0:T(8,128)(2,1)}) custom-call(bf16[448,1024]{1,0:T(8,128)(2,1)} %m_hbm.1, bf16[448,1024]{1,0:T(8,128)(2,1)} %g_hbm.1, bf16[1,16,512]{2,1,0:T(8,128)(2,1)} %f_hbm.1), custom_call_target="tpu_custom_call" | custom-call | tf_op jit(solution)/shard_map/dion_step/pallas_call | solution.py:556
  118.3 3.9 %finish.1 = (bf16[448,1024]{1,0:T(8,128)(2,1)}, bf16[448,1024]{1,0:T(8,128)(2,1)}, bf16[1,16,512]{2,1,0:T(8,128)(2,1)}) custom-call(bf16[448,1024]{1,0:T(8,128)(2,1)} %get-tuple-element.11.b_ref, bf16[448,1024]{1,0:T(8,128)(2,1)} %w_ref.1, bf16[448,512]{1,0:T(8,128)(2,1)} %get-tuple-element.12.lh_ref, bf16[448,512]{1,0:T(8,128)(2,1)} %get-tuple-element.13.sc_ref, ...), custom_call_target="tpu_custom_call" | custom-call | tf_op jit(solution)/shard_map/finish/pallas_call | solution.py:594

commit v5 on v4

--- a/solution.py
+++ b/solution.py
@@ -523,6 +523,9 @@
     lh_v[...] = left.astype(BF16)
     store(lh_v, lh_hbm, 4)
 
+    for copies in (fy, fx, fc, up, down, sg_up, sg_down, gc, gx, gy, gz, hy, hx, hc, *pc, *px, *py, *qy, *qx, *qc):
+        for k in copies:
+            k.wait_send()
     landed(nz)
     total = nz_v[0]
     for d in range(1, NZ):
@@ -534,9 +537,8 @@
     fo_v[0] = (pr_v[pl.ds(pl.multiple_of(i * SHARE, SHARE), SHARE), :] * inv).astype(BF16)
     store(fo_v, fo_hbm, 7)
 
-    for copies in (fy, fx, fc, up, down, sg_up, sg_down, gc, gx, gy, gz, hy, hx, hc, *pc, *px, *py, *qy, *qx, *qc, nz):
-        for k in copies:
-            k.wait_send()
+    for k in nz:
+        k.wait_send()
     for k in stores:
         k.wait()
 

time: 122 us -> 122 us (level)
  no operation moved by 1% of the time
where the time goes in v5:
time: 122 us
  Pallas kernels  122 us (100%)
    pallas_call x1, Pallas kernels, local(): pl.pallas_call(kernel, out_shape=(jax.ShapeDtypeStruct((ROWS, COLS), BF16...  118 us
    pallas_call x1, Pallas kernels, local(): pl.pallas_call(finish, grid=(COLS // tile,), out_shape=(jax.ShapeDtypeStr...  3.94 us

profile of v5, /device:TPU:1, one launch (start us, length us, event | category | flops | bytes accessed | tf_op | source)
XLA Modules:
  0.0 122.3 jit_solution(2835959798424287298)
XLA Ops:
  0.6 117.7 %dion_step.1 = (bf16[448,1024]{1,0:T(8,128)(2,1)}, bf16[448,512]{1,0:T(8,128)(2,1)}, bf16[448,512]{1,0:T(8,128)(2,1)}, bf16[1024,512]{1,0:T(8,128)(2,1)}, bf16[1,16,512]{2,1,0:T(8,128)(2,1)}) custom-call(bf16[448,1024]{1,0:T(8,128)(2,1)} %m_hbm.1, bf16[448,1024]{1,0:T(8,128)(2,1)} %g_hbm.1, bf16[1,16,512]{2,1,0:T(8,128)(2,1)} %f_hbm.1), custom_call_target="tpu_custom_call" | custom-call | tf_op jit(solution)/shard_map/dion_step/pallas_call | solution.py:558
  118.3 3.9 %finish.1 = (bf16[448,1024]{1,0:T(8,128)(2,1)}, bf16[448,1024]{1,0:T(8,128)(2,1)}, bf16[1,16,512]{2,1,0:T(8,128)(2,1)}) custom-call(bf16[448,1024]{1,0:T(8,128)(2,1)} %get-tuple-element.11.b_ref, bf16[448,1024]{1,0:T(8,128)(2,1)} %w_ref.1, bf16[448,512]{1,0:T(8,128)(2,1)} %get-tuple-element.12.lh_ref, bf16[448,512]{1,0:T(8,128)(2,1)} %get-tuple-element.13.sc_ref, ...), custom_call_target="tpu_custom_call" | custom-call | tf_op jit(solution)/shard_map/finish/pallas_call | solution.py:596
